TPU v7x, 512 devices: a whole 4x8x8 slice. The times are simulated.
512 devices in a mesh: blk: 32 (over x, y), pair: 16 (over z, core).
Axes of the slice: x: 4, y: 8, z: 8, core: 2. Of those that a mesh axis runs over, the one named last changes fastest.
Arguments:
- density: bfloat16 [96, 3, 128, 128], P('blk', None, 'pair'), may hold values from -6 to 6
- exponents: float32 [12288], replicated, may hold values from 0.1 to 1
- offsets: float32 [12288], replicated, may hold values from -3 to 3
- expansion: float32 [4, 12288], replicated, may hold values from -6 to 6
- quartet_list: int32 [32, 16, 4, 128], P('blk', 'pair'), may hold values from 0 to 95, as said below
- list_length: int32 [32, 16], P('blk', 'pair'), may hold values from 16 to 128, as said below
Outputs:
- exchange: float32 [96, 3, 128, 128], P('blk', None, 'pair')
Inputs may be any that keep to these rules, and one draw needn't show every extreme that they name: `quartet_list`: every slot holds a quartet: the I of device (b, q) lies in blocks b * 3 to (b + 1) * 3 - 1, and |I - J|, |I - K|, |J - L|, |K - L| are each at most 1. Device (b, q) has the live quartets in its first list_length[b, q] slots; in every draw some device's list is full.
All inputs are finite; a program needn't handle non-finite values.
Results may differ from a plain program's by a relative error of at most 0.0047.
Values may be sent and summed in bfloat16 or wider, within the bound.
No kernel may reach another device: no remote copies, remote signals or barrier semaphores. Data moves between devices by JAX's collectives and lax.ppermute only.
A program may use at most 64 MiB of HBM per device.

v0:
```python
import jax
import jax.numpy as jnp
from jax import lax
from jax.sharding import PartitionSpec as P

BS = 128
W = 1


exchange_scale = 0.0078125


def extended(block, sides, width):
    for axis, dim in sides:
        count = lax.axis_size(axis)
        forward = [(i, i + 1) for i in range(count - 1)]
        backward = [(target, source) for source, target in forward]
        low = lax.ppermute(
            lax.slice_in_dim(block, block.shape[dim] - width, None, axis=dim), axis, forward
        )
        high = lax.ppermute(lax.slice_in_dim(block, 0, width, axis=dim), axis, backward)
        block = jnp.concatenate([low, block, high], axis=dim)
    return block


def block_factors(rows_blk, cols_blk, row_tables, col_tables):
    row_expo = jnp.take(row_tables[0], rows_blk, axis=0)
    column_expo = jnp.take(col_tables[0], cols_blk, axis=0)
    row_position = 2.0 * rows_blk.astype(jnp.float32)[:, None] + jnp.take(
        row_tables[1], rows_blk, axis=0
    )
    column_position = 2.0 * cols_blk.astype(jnp.float32)[:, None] + jnp.take(
        col_tables[1], cols_blk, axis=0
    )
    reduced = (
        row_expo[:, :, None]
        * column_expo[:, None, :]
        / (row_expo[:, :, None] + column_expo[:, None, :])
    )
    distance = row_position[:, :, None] - column_position[:, None, :]
    intersection = jnp.exp(-reduced * distance * distance)
    row_weight = jnp.moveaxis(jnp.take(row_tables[2], rows_blk, axis=1), 0, 1)
    column_weight = jnp.moveaxis(jnp.take(col_tables[2], cols_blk, axis=1), 0, 1)
    mixed = intersection[:, None] * jnp.tanh(
        row_weight[:, :, :, None] * column_weight[:, :, None, :]
    )
    return mixed.astype(jnp.bfloat16)


def shards(density, exponents, offsets, expansion, quartet_list, list_length):
    blocks_here = density.shape[0]
    band_count = density.shape[1]
    expo_table = exponents.reshape(-1, BS)
    offset_table = offsets.reshape(-1, BS)
    weight_table = expansion.reshape(expansion.shape[0], -1, BS)
    col_tables = (expo_table, offset_table, weight_table)
    gathered = lax.all_gather(density, "pair", axis=2, tiled=True)
    nearby = extended(gathered, (("blk", 0),), W)
    tile_bank = nearby.reshape(-1, BS, BS)
    own_first = lax.axis_index("blk") * blocks_here
    first_block = own_first - W
    lane_index = jnp.arange(8, dtype=jnp.int32)
    quartets = quartet_list[0, 0]
    live_count = list_length[0, 0]

    def visit_batch(batch_turn, running):
        selected = lax.dynamic_slice_in_dim(quartets, batch_turn * 8, 8, 1)
        row_block = selected[0]
        col_block = selected[1]
        mid_block = selected[2]
        far_block = selected[3]
        left_factor = block_factors(row_block, mid_block, col_tables, col_tables)
        right_factor = block_factors(col_block, far_block, col_tables, col_tables)
        density_tile = jnp.take(
            tile_bank, (mid_block - first_block) * band_count + far_block - mid_block + W, axis=0
        )
        half_product = jnp.einsum(
            "qpik,qkl->qpil", left_factor, density_tile, preferred_element_type=jnp.float32
        ).astype(jnp.bfloat16)
        quartet_term = jnp.einsum(
            "qpil,qpjl->qij", half_product, right_factor, preferred_element_type=jnp.float32
        )
        alive_mask = (batch_turn * 8 + lane_index < live_count).astype(jnp.float32)
        target = (row_block - own_first) * band_count + col_block - row_block + W
        return running.at[target].add(quartet_term * alive_mask[:, None, None])

    start = jnp.zeros((blocks_here * band_count, BS, BS), jnp.float32)
    partial_value = lax.fori_loop(0, (live_count + 7) // 8, visit_batch, start)
    summed = lax.psum_scatter(
        partial_value.reshape(blocks_here, band_count, BS, BS),
        "pair",
        scatter_dimension=2,
        tiled=True,
    )
    return summed * exchange_scale


def solution(mesh):
    return jax.shard_map(
        shards,
        mesh=mesh,
        in_specs=(
            P("blk", None, "pair", None),
            P(),
            P(),
            P(),
            P("blk", "pair", None, None),
            P("blk", "pair"),
        ),
        out_specs=P("blk", None, "pair", None),
        check_vma=False,
    )
```

profile of v0, /device:TPU:7, one launch (start us, length us, event | category | flops | bytes accessed | tf_op | source)
XLA Modules:
  0.0 355.4 jit_solution(721215304275480671)
XLA Ops:
  6.5 24.7 %all_gather.3 = bf16[3,3,128,128]{3,2,1,0:T(8,128)(2,1)S(1)} all-gather(bf16[3,3,8,128]{3,2,1,0:T(8,128)(2,1)} %param.12), channel_id=1, replica_groups=mesh['blk'=32,'pair'=16] {'pair'}, dimensions={2}, use_global_device_ids=true | all-gather | bytes 313344 | tf_op jit(solution)/shard_map/all_gather | solution.py:57
  31.3 3.2 collective-permute-start
  34.5 4.2 %collective-permute-start.1 = (bf16[1,3,128,128]{3,2,1,0:T(8,128)(2,1)S(1)}, bf16[1,3,128,128]{3,2,1,0:T(8,128)(2,1)S(1)}, u32[]{:S(2)}, u32[]{:S(2)}) collective-permute-start(bf16[1,3,128,128]{3,2,1,0:T(8,128)(2,1)S(1)} %get-tuple-element.240), channel_id=1, source_target_pairs={{16,0},{32,16},{48,32},{64,48},{80,64},{96,80},{112,96},{128,112},... | collective-permute-start | bytes 294920 | tf_op jit(solution)/shard_map/ppermute | solution.py:21
  40.4 173.1 %while.13 = (s32[]{:T(128)}, f32[9,128,128]{2,1,0:T(8,128)S(1)}, s32[]{:T(128)}, s32[4,128]{1,0:T(4,128)S(1)}, s32[]{:T(128)}, /*index=5*/f32[96,128]{1,0:T(8,12...) while((s32[]{:T(128)}, f32[9,128,128]{2,1,0:T(8,128)S(1)}, ...), condition=%wide.region_2.5_spmd.clone, body=%wide.region_0.4_spmd.clone.sunk | while | flops 274368000 | bytes 5494819 | solution.py:88
  47.6 1.5 gather_fusion.1
  49.2 1.5 gather_fusion.6
  50.8 1.5 gather_fusion.7
  63.4 1.5 gather_fusion.1
  65.0 1.5 gather_fusion.6
  66.5 1.5 gather_fusion.7
  79.1 1.5 gather_fusion.1
  82.3 1.5 gather_fusion.7
  94.8 1.5 gather_fusion.1
  96.4 1.5 gather_fusion.6
  98.0 1.5 gather_fusion.7
  110.6 1.5 gather_fusion.1
  113.7 1.5 gather_fusion.7
  126.3 1.5 gather_fusion.1
  129.5 1.5 gather_fusion.7
  142.1 1.5 gather_fusion.1
  145.2 1.5 gather_fusion.7
  159.4 1.5 gather_fusion.6
  161.0 1.5 gather_fusion.7
  173.5 1.5 gather_fusion.1
  175.1 1.5 gather_fusion.6
  176.7 1.5 gather_fusion.7
  189.3 1.5 gather_fusion.1
  190.9 1.5 gather_fusion.6
  192.4 1.5 gather_fusion.7
  205.0 1.5 gather_fusion.1
  208.2 1.5 gather_fusion.7
  214.4 132.7 %reduce-scatter.2.cloned.1.call-done = f32[3,3,8,128]{3,2,1,0:T(8,128)} async-done(((f32[3,3,128,128]{3,2,1,0:T(8,128)}), f32[3,3,8,128]{3,2,1,0:T(8,128)}) %reduce-scatter.2.cloned.1.call-update) | async-done | bytes 36880 | tf_op jit(solution)/shard_map/reduce_scatter | solution.py:89
  (363 shorter events, 134.2 us)
Async XLA Ops:
  6.5 340.6 %reduce-scatter.2.cloned.1.call-start = ((), (), s32[]{:S(2)}) async-start(), calls=%async_computation.1 | async-start | bytes 626688 | tf_op jit(solution)/shard_map/reduce_scatter | solution.py:89
  31.3 8.2 %collective-permute-start = (bf16[1,3,128,128]{3,2,1,0:T(8,128)(2,1)S(1)}, bf16[1,3,128,128]{3,2,1,0:T(8,128)(2,1)S(1)}, u32[]{:S(2)}, u32[]{:S(2)}) collective-permute-start(bf16[1,3,128,128]{3,2,1,0:T(8,128)(2,1)S(1)} %get-tuple-element.239), channel_id=1, source_target_pairs={{0,16},{16,32},{32,48},{48,64},{64,80},{80,96},{96,112},{112,128},... | collective-permute-start | bytes 294920 | tf_op jit(solution)/shard_map/ppermute | solution.py:18
  34.5 5.8 %collective-permute-start.1 = (bf16[1,3,128,128]{3,2,1,0:T(8,128)(2,1)S(1)}, bf16[1,3,128,128]{3,2,1,0:T(8,128)(2,1)S(1)}, u32[]{:S(2)}, u32[]{:S(2)}) collective-permute-start(bf16[1,3,128,128]{3,2,1,0:T(8,128)(2,1)S(1)} %get-tuple-element.240), channel_id=1, source_target_pairs={{16,0},{32,16},{48,32},{64,48},{80,64},{96,80},{112,96},{128,112},... | collective-permute-start | bytes 294920 | tf_op jit(solution)/shard_map/ppermute | solution.py:21
  39.3 1.1 copy-start.1
  39.3 1.1 copy-start.2
  39.4 1.1 copy-start.3
  213.6 0.8 copy-start
Sparse Core Ops, SparseCore 0:
  214.5 132.5 reduce-scatter.1
where the time goes:
time: 360 us; the launch traced here: 355 us
  waiting for transfers between devices  134 us (37%)
  local copies, waits for them, and re-layouts  123 us (34%)
  other arithmetic  34.7 us (10%)
  blocking collectives  24.7 us (7%)
  matrix products  15.9 us (4%)
  between operations  14.2 us (4%)
  starting transfers between devices  7.39 us (2%)
    reduce_scatter x1, waiting for transfers between devices, shards(): lax.psum_scatter(partial_value.reshape(blocks_here, band_count, BS, BS),...  133 us
    gather x22, local copies, waits for them, and re-layouts, block_factors(): row_weight = jnp.moveaxis(jnp.take(row_tables[2], rows_blk, axis=1), 0, 1)  33.1 us
    gather x22, local copies, waits for them, and re-layouts, block_factors(): jnp.take(col_tables[2], cols_blk, axis=1)  33.1 us
    all_gather x1, blocking collectives, shards(): gathered = lax.all_gather(density, 'pair', axis=2, tiled=True)  24.7 us
    dot_general x11, matrix products, visit_batch(): jnp.einsum('qpil,qpjl->qij', half_product, right_factor, preferred_elemen...  15.9 us
    gather x22, local copies, waits for them, and re-layouts, block_factors(): jnp.take(col_tables[1], cols_blk, axis=0)  12.2 us
    gather x22, local copies, waits for them, and re-layouts, block_factors(): row_expo = jnp.take(row_tables[0], rows_blk, axis=0)  12.2 us
    gather x22, local copies, waits for them, and re-layouts, block_factors(): column_expo = jnp.take(col_tables[0], cols_blk, axis=0)  12.2 us
  transfers between devices with their start and end apart: 3, of which 3 were waited for; matrix products, arithmetic and copies ran while one was open for 0% of the time, Pallas kernels for 0%

commit v1 on v0

v1 whole, which is shorter than its diff:
```python
import jax
import jax.numpy as jnp
from jax import lax
from jax.experimental import pallas as pl
from jax.experimental.pallas import tpu as pltpu
from jax.sharding import PartitionSpec as P

BS = 128
NAUX = 4
OWN = 3
BAND = 3
NEAR = OWN + 2
FAR = OWN + 4
ROWS = 8
SCALE = 0.0078125

LEFT_PAIRS = [(k, i) for k in range(NEAR) for i in range(OWN) if abs(i - (k - 1)) <= 1]
FIRST_LEFT = {pair: at for at, pair in enumerate(LEFT_PAIRS)}


def owners_of(near):
    return [i for i in range(OWN) if abs(i - (near - 1)) <= 1]


def factors_kernel(table_ref, list_ref, density_ref, right_ref, left_ref, own_ref, rows_ref, cols_ref):
    own_first = lax.axis_index("blk") * OWN
    my_row = pl.multiple_of(lax.axis_index("pair") * ROWS, ROWS)
    nblk = table_ref.shape[1] // BS

    rows_ref[...] = jnp.zeros_like(rows_ref)
    for t in range(FAR):
        block = jnp.clip(own_first - 2 + t, 0, nblk - 1)
        values = table_ref[:, pl.ds(pl.multiple_of(block * BS, BS), BS)]
        rows_ref[t : t + 1, :] = values[0:1, :]
        rows_ref[8 + t : 9 + t, :] = 2.0 * block.astype(jnp.float32) + values[1:2, :]
        for p in range(NAUX):
            rows_ref[16 + 8 * p + t : 17 + 8 * p + t, :] = values[2 + p : 3 + p, :]
    cols_ref[...] = rows_ref[...].T

    def tiles(columns, t_row, t_col):
        def column(quantity):
            at = 8 * quantity + t_row
            return columns[:, at : at + 1]

        def row(quantity):
            at = 8 * quantity + t_col
            return rows_ref[at : at + 1, :]

        e_r, e_c = column(0), row(0)
        reduced = e_r * e_c / (e_r + e_c)
        distance = column(1) - row(1)
        overlap = jnp.exp(-reduced * distance * distance)
        return [
            (overlap * jnp.tanh(column(2 + p) * row(2 + p))).astype(jnp.bfloat16)
            for p in range(NAUX)
        ]

    step = 32
    for t_far in range(FAR):
        for start in range(0, BS, step):
            columns = cols_ref[start : start + step, :]
            for near in range(NEAR):
                side = t_far - near
                if 0 <= side <= 2:
                    for p, tile in enumerate(tiles(columns, t_far, near + 1)):
                        at = (side * NAUX + p) * BS + start
                        right_ref[near, at : at + step, :] = tile

    mine = cols_ref[pl.ds(my_row, ROWS), :]
    for at, (near, own) in enumerate(LEFT_PAIRS):
        made = tiles(mine, own + 2, near + 1)
        left_ref[at * 32 : at * 32 + 32, :] = jnp.concatenate(made, axis=0)

    row_b, col_b, mid_b, far_b, length = (list_ref[n : n + 1, :] for n in range(5))
    code = (
        (row_b - own_first) * 27 + (col_b - row_b + 1) * 9 + (mid_b - row_b + 1) * 3 + far_b - mid_b + 1
    )
    slot = lax.broadcasted_iota(jnp.int32, (1, BS), 1)
    code = jnp.where(slot < length, code, BS)
    same = code == lax.broadcasted_iota(jnp.int32, (BS, BS), 0)
    first = lax.broadcasted_iota(jnp.int32, (ROWS, BS), 0) == 0
    counts = lax.dot_general(
        first.astype(jnp.float32).astype(jnp.bfloat16),
        same.astype(jnp.float32).astype(jnp.bfloat16),
        (((1,), (1,)), ((), ())),
        preferred_element_type=jnp.float32,
    )
    own_ref[OWN * BAND] = counts.astype(jnp.bfloat16)
    for tile in range(OWN * BAND):
        own_ref[tile] = density_ref[tile // BAND, tile % BAND]


def products_kernel(bank_ref, right_ref, left_ref, out_ref, half_ref, times_ref, mixed_ref):
    def bank(tile):
        return bank_ref[:, tile].astype(jnp.float32).reshape(BS, BS)

    totals = jnp.sum(bank(NEAR * BAND), axis=0, keepdims=True)
    times_ref[...] = jnp.broadcast_to(totals, (BS, BS)).T

    for near in range(NEAR):
        density = jnp.concatenate([bank(near * BAND + c) for c in range(BAND)], axis=1)
        density = density.astype(jnp.bfloat16)
        owners = owners_of(near)
        at = FIRST_LEFT[(near, owners[0])] * 32
        size = len(owners) * 32
        half = jnp.dot(left_ref[at : at + size, :], density, preferred_element_type=jnp.float32)
        half_ref[at : at + size, :] = half.astype(jnp.bfloat16).astype(jnp.float32)

    for j in range(NEAR):
        owners = owners_of(j)
        for slot, i in enumerate(owners):
            for side in range(3):
                far = j - 1 + side
                total = [None] * NAUX
                for k in range(i, i + 3):
                    if abs(far - k) > 1:
                        continue
                    code = i * 27 + (j - i) * 9 + (k - i) * 3 + far - k + 1
                    times = times_ref[code : code + 1, :]
                    at = FIRST_LEFT[(k, i)] * 32
                    column = (far - k + 1) * BS
                    for p in range(NAUX):
                        piece = times * half_ref[
                            at + p * ROWS : at + (p + 1) * ROWS, column : column + BS
                        ]
                        total[p] = piece if total[p] is None else total[p] + piece
                for p in range(NAUX):
                    high = total[p].astype(jnp.bfloat16)
                    low = total[p] - high.astype(jnp.float32)
                    both = jnp.concatenate([high.astype(jnp.float32), low], axis=0)
                    column = (side * NAUX + p) * BS
                    mixed_ref[slot * 16 : slot * 16 + 16, column : column + BS] = both.astype(
                        jnp.bfloat16
                    )
        size = len(owners) * 16
        term = jnp.dot(mixed_ref[:size, :], right_ref[j], preferred_element_type=jnp.float32)
        for slot, i in enumerate(owners):
            pair = term[slot * 16 : slot * 16 + 8] + term[slot * 16 + 8 : slot * 16 + 16]
            out_ref[i, j - i] = pair * SCALE


def vmem(count):
    return [pl.BlockSpec(memory_space=pltpu.VMEM)] * count


def shards(density, exponents, offsets, expansion, quartet_list, list_length):
    count = lax.axis_size("blk")
    forward = [(i, i + 1) for i in range(count - 1)]
    backward = [(i + 1, i) for i in range(count - 1)]
    low = lax.ppermute(density, "blk", forward)[OWN - 1]
    high = lax.ppermute(density, "blk", backward)[0]

    tables = jnp.concatenate([exponents[None], offsets[None], expansion], axis=0)
    listed = jnp.concatenate([quartet_list[0, 0], jnp.broadcast_to(list_length, (1, BS))], axis=0)
    right, left, own = pl.pallas_call(
        factors_kernel,
        out_shape=(
            jax.ShapeDtypeStruct((NEAR, 3 * NAUX * BS, BS), jnp.bfloat16),
            jax.ShapeDtypeStruct((len(LEFT_PAIRS) * NAUX * ROWS, BS), jnp.bfloat16),
            jax.ShapeDtypeStruct((OWN * BAND + 1, ROWS, BS), jnp.bfloat16),
        ),
        in_specs=vmem(3),
        out_specs=tuple(vmem(3)),
        scratch_shapes=[pltpu.VMEM((BS, BS), jnp.float32), pltpu.VMEM((BS, BS), jnp.float32)],
        compiler_params=pltpu.CompilerParams(vmem_limit_bytes=24 * 2**20),
        cost_estimate=pl.CostEstimate(flops=30_000_000, bytes_accessed=3_000_000, transcendentals=1_500_000),
        name="factors",
    )(tables, listed, density)

    payload = jnp.concatenate([low, own[: OWN * BAND], high, own[OWN * BAND :]], axis=0)
    pairs = lax.axis_size("pair")
    copies = jnp.broadcast_to(payload[None], (pairs,) + payload.shape)
    bank = lax.all_to_all(copies, "pair", split_axis=0, concat_axis=0, tiled=True)

    return pl.pallas_call(
        products_kernel,
        out_shape=jax.ShapeDtypeStruct((OWN, BAND, ROWS, BS), jnp.float32),
        in_specs=vmem(3),
        out_specs=pl.BlockSpec(memory_space=pltpu.VMEM),
        scratch_shapes=[
            pltpu.VMEM((len(LEFT_PAIRS) * NAUX * ROWS, BAND * BS), jnp.float32),
            pltpu.VMEM((BS, BS), jnp.float32),
            pltpu.VMEM((3 * 16, 3 * NAUX * BS), jnp.bfloat16),
        ],
        compiler_params=pltpu.CompilerParams(vmem_limit_bytes=24 * 2**20),
        name="products",
    )(bank, right, left)


def solution(mesh):
    return jax.shard_map(
        shards,
        mesh=mesh,
        in_specs=(
            P("blk", None, "pair", None),
            P(),
            P(),
            P(),
            P("blk", "pair", None, None),
            P("blk", "pair"),
        ),
        out_specs=P("blk", None, "pair", None),
        check_vma=False,
    )
```

time: 360 us -> 42.1 us (0.12); the launches traced: 355 us -> 41.9 us
  waiting for transfers between devices: 134 us -> 0.01 us
  local copies, waits for them, and re-layouts: 123 us -> 1.52 us
  other arithmetic: 34.7 us -> 1.1 us
  matrix products: 15.9 us -> 0 us
  between operations: 14.2 us -> 0.74 us
  blocking collectives: 24.7 us -> 28.7 us
    reduce_scatter x1 -> x0, waiting for transfers between devices: 133 us -> none  [shards(): lax.psum_scatter(partial_value.reshape(blocks_here, band_count, BS, BS),...]
    gather x143 -> x0, local copies, waits for them, and re-layouts: 122 us -> none  [the longest x22 33.1 us: block_factors(): row_weight = jnp.moveaxis(jnp.take(row_tables[2], rows_blk, axis=1), 0, 1)]
    all_to_all x0 -> x1, blocking collectives: none -> 28.7 us  [shards(): lax.all_to_all(copies, 'pair', split_axis=0, concat_axis=0, tiled=True)]
    all_gather x1 -> x0, blocking collectives: 24.7 us -> none  [shards(): gathered = lax.all_gather(density, 'pair', axis=2, tiled=True)]
    dot_general x11 -> x0, matrix products: 15.9 us -> none  [visit_batch(): jnp.einsum('qpil,qpjl->qij', half_product, right_factor, preferred_elemen...]
    scatter-add x11 -> x0, other arithmetic: 11.3 us -> none  [visit_batch(): return running.at[target].add(quartet_term * alive_mask[:, None, None])]
    exp x22 -> x0, other arithmetic: 7.56 us -> none  [block_factors(): intersection = jnp.exp(-reduced * distance * distance)]
    and x11 -> x0, other arithmetic: 7.27 us -> none  [block_factors(): row_expo = jnp.take(row_tables[0], rows_blk, axis=0)]
  transfers between devices with their start and end apart: 3 -> 2, of which waited for: 3 -> 0; matrix products, arithmetic and copies ran while one was open for 0% -> 4% of each run, Pallas kernels for 0% -> 3%
where the time goes in v1:
time: 42.1 us; the launch traced here: 41.9 us
  blocking collectives  28.7 us (68%)
  starting transfers between devices  7.38 us (18%)
  Pallas kernels  2.43 us (6%)
  local copies, waits for them, and re-layouts  1.52 us (4%)
  other arithmetic  1.1 us (3%)
  between operations  0.74 us (2%)
    all_to_all x1, blocking collectives, shards(): lax.all_to_all(copies, 'pair', split_axis=0, concat_axis=0, tiled=True)  28.7 us
    ppermute x1, starting transfers between devices, shards(): high = lax.ppermute(density, 'blk', backward)[0]  4.19 us
    ppermute x1, starting transfers between devices, shards(): low = lax.ppermute(density, 'blk', forward)[OWN - 1]  3.19 us
    pallas_call x1, Pallas kernels, shards(): pl.pallas_call(factors_kernel, out_shape=(jax.ShapeDtypeStruct((NEAR, 3 *...  1.25 us
    pallas_call x1, Pallas kernels, shards(): pl.pallas_call(products_kernel, out_shape=jax.ShapeDtypeStruct((OWN, BAND...  1.19 us
    concatenate x1, other arithmetic, shards(): jnp.concatenate([exponents[None], offsets[None], expansion], axis=0)  1.09 us
  transfers between devices with their start and end apart: 2, of which 0 were waited for; matrix products, arithmetic and copies ran while one was open for 4% of the time, Pallas kernels for 3%

profile of v1, /device:TPU:7, one launch (start us, length us, event | category | flops | bytes accessed | tf_op | source)
XLA Modules:
  0.0 41.9 jit_solution(9065528298006399136)
XLA Ops:
  0.0 3.2 %collective-permute-start = (bf16[3,3,8,128]{3,2,1,0:T(8,128)(2,1)}, bf16[3,3,8,128]{3,2,1,0:T(8,128)(2,1)S(1)}, u32[]{:S(2)}, u32[]{:S(2)}) collective-permute-start(bf16[3,3,8,128]{3,2,1,0:T(8,128)(2,1)} %density_ref.1), channel_id=1, source_target_pairs={{0,16},{16,32},{32,48},{48,64},{64,80},{80,96},{96,112},{112,128},... | collective-permute-start | bytes 55304 | tf_op jit(solution)/shard_map/ppermute | solution.py:150
  3.2 4.2 %collective-permute-start.1 = (bf16[3,3,8,128]{3,2,1,0:T(8,128)(2,1)}, bf16[3,3,8,128]{3,2,1,0:T(8,128)(2,1)S(1)}, u32[]{:S(2)}, u32[]{:S(2)}) collective-permute-start(bf16[3,3,8,128]{3,2,1,0:T(8,128)(2,1)} %density_ref.1), channel_id=1, source_target_pairs={{16,0},{32,16},{48,32},{64,48},{80,64},{96,80},{112,96},{128,112},... | collective-permute-start | bytes 55304 | tf_op jit(solution)/shard_map/ppermute | solution.py:151
  7.4 1.1 %pad_maximum_fusion.table_ref = f32[6,12288]{1,0:T(8,128)S(1)} fusion(f32[4,12288]{1,0:T(4,128)} %param.9, f32[1,12288]{1,0:T(1,128)} %bitcast.9, f32[1,12288]{1,0:T(1,128)} %bitcast.10), kind=kLoop, calls=%fused_computation | loop fusion | flops 147456 | bytes 589824 | tf_op jit(solution)/shard_map/concatenate | solution.py:153
  9.1 0.7 %concatenate.10.list_ref = s32[5,128]{1,0:T(8,128)S(1)} pad(s32[4,128]{1,0:T(4,128)} %bitcast.11, s32[]{:T(128)} %bitcast.8), padding=0_1x0_0 | pad | bytes 4612 | tf_op jit(solution)/shard_map/concatenate | solution.py:154
  9.8 0.0 copy-start
  9.8 0.7 %copy-done = bf16[3,3,8,128]{3,2,1,0:T(8,128)(2,1)S(1)} copy-done((bf16[3,3,8,128]{3,2,1,0:T(8,128)(2,1)S(1)}, bf16[3,3,8,128]{3,2,1,0:T(8,128)(2,1)}, u32[]{:S(2)}) %copy-start) | copy-done | bytes 18456
  10.6 1.2 %factors.1 = (bf16[5,1536,128]{2,1,0:T(8,128)(2,1)S(1)}, bf16[288,128]{1,0:T(8,128)(2,1)S(1)}, bf16[10,8,128]{2,1,0:T(8,128)(2,1)S(1)}) custom-call(f32[6,12288]{1,0:T(8,128)S(1)} %pad_maximum_fusion.table_ref, s32[5,128]{1,0:T(8,128)S(1)} %concatenate.10.list_ref, bf16[3,3,8,128]{3,2,1,0:T(8,128)(2,1)S(1)} %copy-done), custom_call_target="tpu_custom_call" | custom-call | flops 30000000 | bytes 3000000 | tf_op jit(solution)/shard_map/factors/pallas_call | solution.py:155
  11.8 0.0 collective-permute-done
  11.8 0.0 collective-permute-done.1
  11.9 0.1 broadcast_in_dim.20
  12.0 28.7 %all_to_all.5.bank_ref = bf16[16,16,8,128]{3,2,1,0:T(8,128)(2,1)S(1)} all-to-all(bf16[16,16,8,128]{3,2,1,0:T(8,128)(2,1)S(1)} %broadcast_in_dim.20), channel_id=1, replica_groups=mesh['blk'=32,'pair'=16] {'pair'}, dimensions={0} | all-to-all | bytes 1048576 | tf_op jit(solution)/shard_map/all_to_all | solution.py:173
  40.7 1.2 %products.1 = f32[3,3,8,128]{3,2,1,0:T(8,128)} custom-call(bf16[16,16,8,128]{3,2,1,0:T(8,128)(2,1)S(1)} %all_to_all.5.bank_ref, bf16[5,1536,128]{2,1,0:T(8,128)(2,1)S(1)} %get-tuple-element.9.right_ref, bf16[288,128]{1,0:T(8,128)(2,1)S(1)} %get-tuple-element.10.left_ref), custom_call_target="tpu_custom_call" | custom-call | tf_op jit(solution)/shard_map/products/pallas_call | solution.py:175
  (5 shorter events, 0.0 us)
Async XLA Ops:
  0.0 11.8 %collective-permute-start = (bf16[3,3,8,128]{3,2,1,0:T(8,128)(2,1)}, bf16[3,3,8,128]{3,2,1,0:T(8,128)(2,1)S(1)}, u32[]{:S(2)}, u32[]{:S(2)}) collective-permute-start(bf16[3,3,8,128]{3,2,1,0:T(8,128)(2,1)} %density_ref.1), channel_id=1, source_target_pairs={{0,16},{16,32},{32,48},{48,64},{64,80},{80,96},{96,112},{112,128},... | collective-permute-start | bytes 55304 | tf_op jit(solution)/shard_map/ppermute | solution.py:150
  3.2 8.6 %collective-permute-start.1 = (bf16[3,3,8,128]{3,2,1,0:T(8,128)(2,1)}, bf16[3,3,8,128]{3,2,1,0:T(8,128)(2,1)S(1)}, u32[]{:S(2)}, u32[]{:S(2)}) collective-permute-start(bf16[3,3,8,128]{3,2,1,0:T(8,128)(2,1)} %density_ref.1), channel_id=1, source_target_pairs={{16,0},{32,16},{48,32},{64,48},{80,64},{96,80},{112,96},{128,112},... | collective-permute-start | bytes 55304 | tf_op jit(solution)/shard_map/ppermute | solution.py:151
  9.8 0.7 %copy-start = (bf16[3,3,8,128]{3,2,1,0:T(8,128)(2,1)S(1)}, bf16[3,3,8,128]{3,2,1,0:T(8,128)(2,1)}, u32[]{:S(2)}) copy-start(bf16[3,3,8,128]{3,2,1,0:T(8,128)(2,1)} %density_ref.1) | copy-start | bytes 55300

commit v2 on v1

--- a/solution.py
+++ b/solution.py
@@ -22,7 +22,7 @@
     return [i for i in range(OWN) if abs(i - (near - 1)) <= 1]
 
 
-def factors_kernel(table_ref, list_ref, density_ref, right_ref, left_ref, own_ref, rows_ref, cols_ref):
+def factors_kernel(table_ref, right_ref, left_ref, rows_ref, cols_ref):
     own_first = lax.axis_index("blk") * OWN
     my_row = pl.multiple_of(lax.axis_index("pair") * ROWS, ROWS)
     nblk = table_ref.shape[1] // BS
@@ -71,31 +71,27 @@
         made = tiles(mine, own + 2, near + 1)
         left_ref[at * 32 : at * 32 + 32, :] = jnp.concatenate(made, axis=0)
 
-    row_b, col_b, mid_b, far_b, length = (list_ref[n : n + 1, :] for n in range(5))
-    code = (
-        (row_b - own_first) * 27 + (col_b - row_b + 1) * 9 + (mid_b - row_b + 1) * 3 + far_b - mid_b + 1
-    )
-    slot = lax.broadcasted_iota(jnp.int32, (1, BS), 1)
-    code = jnp.where(slot < length, code, BS)
-    same = code == lax.broadcasted_iota(jnp.int32, (BS, BS), 0)
-    first = lax.broadcasted_iota(jnp.int32, (ROWS, BS), 0) == 0
-    counts = lax.dot_general(
-        first.astype(jnp.float32).astype(jnp.bfloat16),
-        same.astype(jnp.float32).astype(jnp.bfloat16),
-        (((1,), (1,)), ((), ())),
-        preferred_element_type=jnp.float32,
-    )
-    own_ref[OWN * BAND] = counts.astype(jnp.bfloat16)
-    for tile in range(OWN * BAND):
-        own_ref[tile] = density_ref[tile // BAND, tile % BAND]
-
 
 def products_kernel(bank_ref, right_ref, left_ref, out_ref, half_ref, times_ref, mixed_ref):
     def bank(tile):
         return bank_ref[:, tile].astype(jnp.float32).reshape(BS, BS)
 
-    totals = jnp.sum(bank(NEAR * BAND), axis=0, keepdims=True)
-    times_ref[...] = jnp.broadcast_to(totals, (BS, BS)).T
+    own_first = lax.axis_index("blk") * OWN
+    slot = lax.broadcasted_iota(jnp.int32, (1, BS), 1)
+    code_row = lax.broadcasted_iota(jnp.int32, (BS, BS), 0)
+    lists = bank_ref[:, NEAR * BAND].astype(jnp.float32).astype(jnp.int32)
+    found = jnp.zeros((BS, BS), jnp.float32)
+    for q in range(lists.shape[0]):
+        row_b, col_b, mid_b, far_b = (lists[q, n : n + 1, :] for n in range(4))
+        length = lists[q, 4:5, 0:1]
+        code = (
+            (row_b - own_first) * 27 + (col_b - row_b + 1) * 9 + (mid_b - row_b + 1) * 3 + far_b - mid_b + 1
+        )
+        code = jnp.where(slot < length, code, BS)
+        found += (code == code_row).astype(jnp.float32)
+    times_ref[...] = jnp.dot(
+        found.astype(jnp.bfloat16), jnp.ones((BS, BS), jnp.bfloat16), preferred_element_type=jnp.float32
+    )
 
     for near in range(NEAR):
         density = jnp.concatenate([bank(near * BAND + c) for c in range(BAND)], axis=1)
@@ -145,32 +141,37 @@
 
 def shards(density, exponents, offsets, expansion, quartet_list, list_length):
     count = lax.axis_size("blk")
-    forward = [(i, i + 1) for i in range(count - 1)]
-    backward = [(i + 1, i) for i in range(count - 1)]
-    low = lax.ppermute(density, "blk", forward)[OWN - 1]
-    high = lax.ppermute(density, "blk", backward)[0]
+    odd = (lax.axis_index("blk") & 1) == 1
+
+    def exchanged(first):
+        lower = range(first, count - 1, 2)
+        return lax.ppermute(density, "blk", [(i, i + 1) for i in lower] + [(i + 1, i) for i in lower])
+
+    inner, outer = exchanged(0), exchanged(1)
+    low = jnp.where(odd, inner[OWN - 1], outer[OWN - 1])
+    high = jnp.where(odd, outer[0], inner[0])
 
     tables = jnp.concatenate([exponents[None], offsets[None], expansion], axis=0)
-    listed = jnp.concatenate([quartet_list[0, 0], jnp.broadcast_to(list_length, (1, BS))], axis=0)
-    right, left, own = pl.pallas_call(
+    right, left = pl.pallas_call(
         factors_kernel,
         out_shape=(
             jax.ShapeDtypeStruct((NEAR, 3 * NAUX * BS, BS), jnp.bfloat16),
             jax.ShapeDtypeStruct((len(LEFT_PAIRS) * NAUX * ROWS, BS), jnp.bfloat16),
-            jax.ShapeDtypeStruct((OWN * BAND + 1, ROWS, BS), jnp.bfloat16),
         ),
-        in_specs=vmem(3),
-        out_specs=tuple(vmem(3)),
+        in_specs=vmem(1),
+        out_specs=tuple(vmem(2)),
         scratch_shapes=[pltpu.VMEM((BS, BS), jnp.float32), pltpu.VMEM((BS, BS), jnp.float32)],
         compiler_params=pltpu.CompilerParams(vmem_limit_bytes=24 * 2**20),
         cost_estimate=pl.CostEstimate(flops=30_000_000, bytes_accessed=3_000_000, transcendentals=1_500_000),
         name="factors",
-    )(tables, listed, density)
-
-    payload = jnp.concatenate([low, own[: OWN * BAND], high, own[OWN * BAND :]], axis=0)
-    pairs = lax.axis_size("pair")
-    copies = jnp.broadcast_to(payload[None], (pairs,) + payload.shape)
-    bank = lax.all_to_all(copies, "pair", split_axis=0, concat_axis=0, tiled=True)
+    )(tables)
+
+    listed = jnp.pad(quartet_list[0, 0], ((0, ROWS - 4), (0, 0)))
+    listed += jnp.pad(list_length, ((4, ROWS - 5), (0, BS - 1)))
+    payload = jnp.concatenate(
+        [low, density.reshape(OWN * BAND, ROWS, BS), high, listed.astype(jnp.bfloat16)[None]], axis=0
+    )
+    bank = lax.all_gather(payload, "pair", axis=0)
 
     return pl.pallas_call(
         products_kernel,

time: 42.1 us -> 39.5 us (0.938)
  blocking collectives: 28.7 us -> 25.7 us
  local copies, waits for them, and re-layouts: 1.52 us -> 0.01 us
  starting transfers between devices: 7.38 us -> 8.46 us
  other arithmetic: 1.1 us -> 1.81 us
    all_to_all x1 -> x0, blocking collectives: 28.7 us -> none  [shards(): lax.all_to_all(copies, 'pair', split_axis=0, concat_axis=0, tiled=True)]
    all_gather x0 -> x1, blocking collectives: none -> 25.7 us  [shards(): bank = lax.all_gather(payload, 'pair', axis=0)]
    ppermute x2, starting transfers between devices: 7.38 us -> 8.46 us  [exchanged(): lax.ppermute(density, 'blk', [(i, i + 1) for i in lower] + [(i + 1, i) fo...]
    unnamed x2, local copies, waits for them, and re-layouts: 0.72 us -> 0.01 us
    broadcast_in_dim x0 -> x1, other arithmetic: none -> 0.7 us  [shards(): listed.astype(jnp.bfloat16)[None]]
    concatenate x1 -> x0, local copies, waits for them, and re-layouts: 0.69 us -> none  [shards(): jnp.concatenate([quartet_list[0, 0], jnp.broadcast_to(list_length, (1, BS...]
  transfers between devices with their start and end apart: 2 -> 2, of which waited for: 0 -> 0; matrix products, arithmetic and copies ran while one was open for 4% -> 5% of each run, Pallas kernels for 3% -> 3%
where the time goes in v2:
time: 39.5 us; the launch traced here: 39.3 us
  blocking collectives  25.7 us (65%)
  starting transfers between devices  8.46 us (21%)
  Pallas kernels  2.61 us (7%)
  other arithmetic  1.81 us (5%)
  between operations  0.71 us (2%)
    all_gather x1, blocking collectives, shards(): bank = lax.all_gather(payload, 'pair', axis=0)  25.7 us
    ppermute x2, starting transfers between devices, exchanged(): lax.ppermute(density, 'blk', [(i, i + 1) for i in lower] + [(i + 1, i) fo...  8.46 us
    pallas_call x1, Pallas kernels, shards(): pl.pallas_call(products_kernel, out_shape=jax.ShapeDtypeStruct((OWN, BAND...  1.36 us
    pallas_call x1, Pallas kernels, shards(): pl.pallas_call(factors_kernel, out_shape=(jax.ShapeDtypeStruct((NEAR, 3 *...  1.25 us
    concatenate x1, other arithmetic, shards(): jnp.concatenate([exponents[None], offsets[None], expansion], axis=0)  1.09 us
  transfers between devices with their start and end apart: 2, of which 0 were waited for; matrix products, arithmetic and copies ran while one was open for 5% of the time, Pallas kernels for 3%

profile of v2, /device:TPU:7, one launch (start us, length us, event | category | flops | bytes accessed | tf_op | source)
XLA Modules:
  0.0 39.3 jit_solution(15673904934484284842)
XLA Ops:
  0.0 0.0 copy-start
  0.0 3.3 %collective-permute-start = (bf16[3,3,8,128]{3,2,1,0:T(8,128)(2,1)}, bf16[3,3,8,128]{3,2,1,0:T(8,128)(2,1)S(1)}, u32[]{:S(2)}, u32[]{:S(2)}) collective-permute-start(bf16[3,3,8,128]{3,2,1,0:T(8,128)(2,1)} %param.6), channel_id=1, source_target_pairs={{0,16},{32,48},{64,80},{96,112},{128,144},{160,176},{192,208},{224... | collective-permute-start | bytes 55304 | tf_op jit(solution)/shard_map/ppermute | solution.py:148
  3.3 5.1 %collective-permute-start.1 = (bf16[3,3,8,128]{3,2,1,0:T(8,128)(2,1)}, bf16[3,3,8,128]{3,2,1,0:T(8,128)(2,1)S(1)}, u32[]{:S(2)}, u32[]{:S(2)}) collective-permute-start(bf16[3,3,8,128]{3,2,1,0:T(8,128)(2,1)} %param.6), channel_id=1, source_target_pairs={{16,32},{48,64},{80,96},{112,128},{144,160},{176,192},{208,224},{2... | collective-permute-start | bytes 55304 | tf_op jit(solution)/shard_map/ppermute | solution.py:148
  9.1 1.1 %pad_maximum_fusion.table_ref = f32[6,12288]{1,0:T(8,128)S(1)} fusion(f32[4,12288]{1,0:T(4,128)} %param.9, f32[1,12288]{1,0:T(1,128)} %bitcast.12, f32[1,12288]{1,0:T(1,128)} %bitcast.13), kind=kLoop, calls=%fused_computation | loop fusion | flops 147456 | bytes 589824 | tf_op jit(solution)/shard_map/concatenate | solution.py:154
  10.2 0.7 %fusion.2 = bf16[1,8,128]{2,1,0:T(8,128)(2,1)S(1)} fusion(s32[1,1]{1,0:T(1,128)S(6)} %copy.7, s32[4,128]{1,0:T(4,128)} %bitcast.15), kind=kLoop, calls=%fused_computation.7 | loop fusion | flops 2048 | bytes 4100 | tf_op jit(solution)/shard_map/broadcast_in_dim | solution.py:172
  10.9 1.3 %factors.1 = (bf16[5,1536,128]{2,1,0:T(8,128)(2,1)S(1)}, bf16[288,128]{1,0:T(8,128)(2,1)S(1)}) custom-call(f32[6,12288]{1,0:T(8,128)S(1)} %pad_maximum_fusion.table_ref), custom_call_target="tpu_custom_call" | custom-call | flops 30000000 | bytes 3000000 | tf_op jit(solution)/shard_map/factors/pallas_call | solution.py:155
  12.2 0.0 collective-permute-done
  12.2 0.0 collective-permute-done.1
  12.2 0.0 copy-done
  12.2 25.7 %all-gather = bf16[256,8,128]{2,1,0:T(8,128)(2,1)S(1)} all-gather(bf16[16,8,128]{2,1,0:T(8,128)(2,1)S(1)} %pad_maximum_fusion.1), channel_id=2, replica_groups=mesh['blk'=32,'pair'=16] {'pair'}, dimensions={0}, use_global_device_ids=true | all-gather | bytes 557056 | tf_op jit(solution)/shard_map/all_gather | solution.py:174
  37.9 1.4 %products.1 = f32[3,3,8,128]{3,2,1,0:T(8,128)} custom-call(bf16[16,16,8,128]{3,2,1,0:T(8,128)(2,1)S(1)} %bitcast.11, bf16[5,1536,128]{2,1,0:T(8,128)(2,1)S(1)} %get-tuple-element.7.right_ref, bf16[288,128]{1,0:T(8,128)(2,1)S(1)} %get-tuple-element.8.left_ref), custom_call_target="tpu_custom_call" | custom-call | tf_op jit(solution)/shard_map/products/pallas_call | solution.py:176
  (2 shorter events, 0.0 us)
Async XLA Ops:
  0.0 12.2 %copy-start = (bf16[3,3,8,128]{3,2,1,0:T(8,128)(2,1)S(1)}, bf16[3,3,8,128]{3,2,1,0:T(8,128)(2,1)}, u32[]{:S(2)}) copy-start(bf16[3,3,8,128]{3,2,1,0:T(8,128)(2,1)} %param.6) | copy-start | bytes 55300
  0.0 12.2 %collective-permute-start = (bf16[3,3,8,128]{3,2,1,0:T(8,128)(2,1)}, bf16[3,3,8,128]{3,2,1,0:T(8,128)(2,1)S(1)}, u32[]{:S(2)}, u32[]{:S(2)}) collective-permute-start(bf16[3,3,8,128]{3,2,1,0:T(8,128)(2,1)} %param.6), channel_id=1, source_target_pairs={{0,16},{32,48},{64,80},{96,112},{128,144},{160,176},{192,208},{224... | collective-permute-start | bytes 55304 | tf_op jit(solution)/shard_map/ppermute | solution.py:148
  3.3 8.8 %collective-permute-start.1 = (bf16[3,3,8,128]{3,2,1,0:T(8,128)(2,1)}, bf16[3,3,8,128]{3,2,1,0:T(8,128)(2,1)S(1)}, u32[]{:S(2)}, u32[]{:S(2)}) collective-permute-start(bf16[3,3,8,128]{3,2,1,0:T(8,128)(2,1)} %param.6), channel_id=1, source_target_pairs={{16,32},{48,64},{80,96},{112,128},{144,160},{176,192},{208,224},{2... | collective-permute-start | bytes 55304 | tf_op jit(solution)/shard_map/ppermute | solution.py:148

commit v3 on v2

--- a/solution.py
+++ b/solution.py
@@ -22,7 +22,11 @@
     return [i for i in range(OWN) if abs(i - (near - 1)) <= 1]
 
 
-def factors_kernel(table_ref, right_ref, left_ref, rows_ref, cols_ref):
+def early():
+    return lax.axis_index("pair") < 4
+
+
+def make_factors(table_ref, right_ref, left_ref, rows_ref, cols_ref):
     own_first = lax.axis_index("blk") * OWN
     my_row = pl.multiple_of(lax.axis_index("pair") * ROWS, ROWS)
     nblk = table_ref.shape[1] // BS
@@ -72,7 +76,27 @@
         left_ref[at * 32 : at * 32 + 32, :] = jnp.concatenate(made, axis=0)
 
 
-def products_kernel(bank_ref, right_ref, left_ref, out_ref, half_ref, times_ref, mixed_ref):
+def factors_kernel(table_ref, right_ref, left_ref, rows_ref, cols_ref):
+    @pl.when(early())
+    def _():
+        make_factors(table_ref, right_ref, left_ref, rows_ref, cols_ref)
+
+
+def products_kernel(
+    bank_ref, table_ref, right_in, left_in, out_ref,
+    half_ref, times_ref, mixed_ref, right_ref, left_ref, rows_ref, cols_ref
+):
+    @pl.when(early())
+    def _():
+        make_products(bank_ref, right_in, left_in, out_ref, half_ref, times_ref, mixed_ref)
+
+    @pl.when(jnp.logical_not(early()))
+    def _():
+        make_factors(table_ref, right_ref, left_ref, rows_ref, cols_ref)
+        make_products(bank_ref, right_ref, left_ref, out_ref, half_ref, times_ref, mixed_ref)
+
+
+def make_products(bank_ref, right_ref, left_ref, out_ref, half_ref, times_ref, mixed_ref):
     def bank(tile):
         return bank_ref[:, tile].astype(jnp.float32).reshape(BS, BS)
 
@@ -141,15 +165,10 @@
 
 def shards(density, exponents, offsets, expansion, quartet_list, list_length):
     count = lax.axis_size("blk")
-    odd = (lax.axis_index("blk") & 1) == 1
-
-    def exchanged(first):
-        lower = range(first, count - 1, 2)
-        return lax.ppermute(density, "blk", [(i, i + 1) for i in lower] + [(i + 1, i) for i in lower])
-
-    inner, outer = exchanged(0), exchanged(1)
-    low = jnp.where(odd, inner[OWN - 1], outer[OWN - 1])
-    high = jnp.where(odd, outer[0], inner[0])
+    forward = [(i, i + 1) for i in range(count - 1)]
+    backward = [(i + 1, i) for i in range(count - 1)]
+    low = lax.ppermute(density, "blk", forward)[OWN - 1]
+    high = lax.ppermute(density, "blk", backward)[0]
 
     tables = jnp.concatenate([exponents[None], offsets[None], expansion], axis=0)
     right, left = pl.pallas_call(
@@ -171,21 +190,26 @@
     payload = jnp.concatenate(
         [low, density.reshape(OWN * BAND, ROWS, BS), high, listed.astype(jnp.bfloat16)[None]], axis=0
     )
+    payload, right, left = lax.optimization_barrier((payload, right, left))
     bank = lax.all_gather(payload, "pair", axis=0)
 
     return pl.pallas_call(
         products_kernel,
         out_shape=jax.ShapeDtypeStruct((OWN, BAND, ROWS, BS), jnp.float32),
-        in_specs=vmem(3),
+        in_specs=vmem(4),
         out_specs=pl.BlockSpec(memory_space=pltpu.VMEM),
         scratch_shapes=[
             pltpu.VMEM((len(LEFT_PAIRS) * NAUX * ROWS, BAND * BS), jnp.float32),
             pltpu.VMEM((BS, BS), jnp.float32),
             pltpu.VMEM((3 * 16, 3 * NAUX * BS), jnp.bfloat16),
+            pltpu.VMEM(right.shape, jnp.bfloat16),
+            pltpu.VMEM(left.shape, jnp.bfloat16),
+            pltpu.VMEM((BS, BS), jnp.float32),
+            pltpu.VMEM((BS, BS), jnp.float32),
         ],
         compiler_params=pltpu.CompilerParams(vmem_limit_bytes=24 * 2**20),
         name="products",
-    )(bank, right, left)
+    )(bank, tables, right, left)
 
 
 def solution(mesh):

time: 39.5 us -> 38.6 us (0.977)
  the two profiles are of different devices: /device:TPU:7 before, /device:TPU:31 now
where the time goes in v3:
time: 38.6 us; the launch traced here: 38.3 us
  blocking collectives  26.5 us (69%)
  starting transfers between devices  6.45 us (17%)
  Pallas kernels  2.56 us (7%)
  other arithmetic  1.79 us (5%)
  between operations  0.69 us (2%)
    all_gather x1, blocking collectives, shards(): bank = lax.all_gather(payload, 'pair', axis=0)  26.5 us
    ppermute x1, starting transfers between devices, shards(): low = lax.ppermute(density, 'blk', forward)[OWN - 1]  4.53 us
    ppermute x1, starting transfers between devices, shards(): high = lax.ppermute(density, 'blk', backward)[0]  1.92 us
    pallas_call x1, Pallas kernels, shards(): pl.pallas_call(products_kernel, out_shape=jax.ShapeDtypeStruct((OWN, BAND...  1.32 us
    pallas_call x1, Pallas kernels, shards(): pl.pallas_call(factors_kernel, out_shape=(jax.ShapeDtypeStruct((NEAR, 3 *...  1.24 us
    concatenate x1, other arithmetic, shards(): jnp.concatenate([exponents[None], offsets[None], expansion], axis=0)  1.09 us
  transfers between devices with their start and end apart: 2, of which 1 were waited for; matrix products, arithmetic and copies ran while one was open for 5% of the time, Pallas kernels for 3%

profile of v3, /device:TPU:31, one launch (start us, length us, event | category | flops | bytes accessed | tf_op | source)
XLA Modules:
  0.0 38.3 jit_solution(15441891653141466238)
XLA Ops:
  0.0 0.0 copy-start
  0.0 4.5 %collective-permute-start = (bf16[3,3,8,128]{3,2,1,0:T(8,128)(2,1)}, bf16[3,3,8,128]{3,2,1,0:T(8,128)(2,1)S(1)}, u32[]{:S(2)}, u32[]{:S(2)}) collective-permute-start(bf16[3,3,8,128]{3,2,1,0:T(8,128)(2,1)} %param.6), channel_id=1, source_target_pairs={{0,16},{16,32},{32,48},{48,64},{64,80},{80,96},{96,112},{112,128},... | collective-permute-start | bytes 55304 | tf_op jit(solution)/shard_map/ppermute | solution.py:170
  4.5 1.9 %collective-permute-start.1 = (bf16[3,3,8,128]{3,2,1,0:T(8,128)(2,1)}, bf16[3,3,8,128]{3,2,1,0:T(8,128)(2,1)S(1)}, u32[]{:S(2)}, u32[]{:S(2)}) collective-permute-start(bf16[3,3,8,128]{3,2,1,0:T(8,128)(2,1)} %param.6), channel_id=1, source_target_pairs={{16,0},{32,16},{48,32},{64,48},{80,64},{96,80},{112,96},{128,112},... | collective-permute-start | bytes 55304 | tf_op jit(solution)/shard_map/ppermute | solution.py:171
  7.1 1.1 %pad_maximum_fusion.table_ref = f32[6,12288]{1,0:T(8,128)S(1)} fusion(f32[4,12288]{1,0:T(4,128)} %param.9, f32[1,12288]{1,0:T(1,128)} %bitcast.12, f32[1,12288]{1,0:T(1,128)} %bitcast.13), kind=kLoop, calls=%fused_computation | loop fusion | flops 147456 | bytes 589824 | tf_op jit(solution)/shard_map/concatenate | solution.py:173
  8.2 0.7 %fusion = bf16[1,8,128]{2,1,0:T(8,128)(2,1)S(1)} fusion(s32[1,1]{1,0:T(1,128)S(6)} %copy.7, s32[4,128]{1,0:T(4,128)} %bitcast.15), kind=kLoop, calls=%fused_computation.5 | loop fusion | flops 2048 | bytes 4100 | tf_op jit(solution)/shard_map/broadcast_in_dim | solution.py:191
  8.9 1.2 %factors.1 = (bf16[5,1536,128]{2,1,0:T(8,128)(2,1)S(1)}, bf16[288,128]{1,0:T(8,128)(2,1)S(1)}) custom-call(f32[6,12288]{1,0:T(8,128)S(1)} %pad_maximum_fusion.table_ref), custom_call_target="tpu_custom_call" | custom-call | flops 30000000 | bytes 3000000 | tf_op jit(solution)/shard_map/factors/pallas_call | solution.py:174
  10.2 0.0 collective-permute-done
  10.2 0.3 collective-permute-done.1
  10.5 0.0 copy-done
  10.5 26.5 %all-gather = bf16[256,8,128]{2,1,0:T(8,128)(2,1)S(1)} all-gather(bf16[16,8,128]{2,1,0:T(8,128)(2,1)S(1)} %pad_maximum_fusion.1), channel_id=2, replica_groups=mesh['blk'=32,'pair'=16] {'pair'}, dimensions={0}, use_global_device_ids=true | all-gather | bytes 557056 | tf_op jit(solution)/shard_map/all_gather | solution.py:194
  37.0 1.3 %products.1 = f32[3,3,8,128]{3,2,1,0:T(8,128)} custom-call(bf16[16,16,8,128]{3,2,1,0:T(8,128)(2,1)S(1)} %bitcast.11, f32[6,12288]{1,0:T(8,128)S(1)} %pad_maximum_fusion.table_ref, bf16[5,1536,128]{2,1,0:T(8,128)(2,1)S(1)} %get-tuple-element.13.right_in, bf16[288,128]{1,0:T(8,128)(2,1)S(1)} %get-tuple-element.14.left_in), custom_call_target="tpu_custom_call" | custom-call | tf_op jit(solution)/shard_map/products/pallas_call | solution.py:196
  (3 shorter events, 0.0 us)
Async XLA Ops:
  0.0 10.5 %copy-start = (bf16[3,3,8,128]{3,2,1,0:T(8,128)(2,1)S(1)}, bf16[3,3,8,128]{3,2,1,0:T(8,128)(2,1)}, u32[]{:S(2)}) copy-start(bf16[3,3,8,128]{3,2,1,0:T(8,128)(2,1)} %param.6) | copy-start | bytes 55300
  0.0 10.2 %collective-permute-start = (bf16[3,3,8,128]{3,2,1,0:T(8,128)(2,1)}, bf16[3,3,8,128]{3,2,1,0:T(8,128)(2,1)S(1)}, u32[]{:S(2)}, u32[]{:S(2)}) collective-permute-start(bf16[3,3,8,128]{3,2,1,0:T(8,128)(2,1)} %param.6), channel_id=1, source_target_pairs={{0,16},{16,32},{32,48},{48,64},{64,80},{80,96},{96,112},{112,128},... | collective-permute-start | bytes 55304 | tf_op jit(solution)/shard_map/ppermute | solution.py:170
  4.5 5.9 %collective-permute-start.1 = (bf16[3,3,8,128]{3,2,1,0:T(8,128)(2,1)}, bf16[3,3,8,128]{3,2,1,0:T(8,128)(2,1)S(1)}, u32[]{:S(2)}, u32[]{:S(2)}) collective-permute-start(bf16[3,3,8,128]{3,2,1,0:T(8,128)(2,1)} %param.6), channel_id=1, source_target_pairs={{16,0},{32,16},{48,32},{64,48},{80,64},{96,80},{112,96},{128,112},... | collective-permute-start | bytes 55304 | tf_op jit(solution)/shard_map/ppermute | solution.py:171

commit v4 on v3

--- a/solution.py
+++ b/solution.py
@@ -97,8 +97,15 @@
 
 
 def make_products(bank_ref, right_ref, left_ref, out_ref, half_ref, times_ref, mixed_ref):
-    def bank(tile):
-        return bank_ref[:, tile].astype(jnp.float32).reshape(BS, BS)
+    devices = bank_ref.shape[0]
+
+    def bank(near, c):
+        if 0 < near < NEAR - 1:
+            pieces = [bank_ref[q, (near - 1) * BAND + c] for q in range(devices)]
+        else:
+            holder = 0 if near == 0 else 1
+            pieces = [bank_ref[q // 2 * 2 + holder, OWN * BAND + 2 * c + q % 2] for q in range(devices)]
+        return jnp.concatenate([piece.astype(jnp.float32) for piece in pieces], axis=0)
 
     own_first = lax.axis_index("blk") * OWN
     slot = lax.broadcasted_iota(jnp.int32, (1, BS), 1)
@@ -118,7 +125,7 @@
     )
 
     for near in range(NEAR):
-        density = jnp.concatenate([bank(near * BAND + c) for c in range(BAND)], axis=1)
+        density = jnp.concatenate([bank(near, c) for c in range(BAND)], axis=1)
         density = density.astype(jnp.bfloat16)
         owners = owners_of(near)
         at = FIRST_LEFT[(near, owners[0])] * 32
@@ -165,10 +172,18 @@
 
 def shards(density, exponents, offsets, expansion, quartet_list, list_length):
     count = lax.axis_size("blk")
-    forward = [(i, i + 1) for i in range(count - 1)]
-    backward = [(i + 1, i) for i in range(count - 1)]
-    low = lax.ppermute(density, "blk", forward)[OWN - 1]
-    high = lax.ppermute(density, "blk", backward)[0]
+    pairs = lax.axis_size("pair")
+    second = (lax.axis_index("pair") & 1) == 1
+
+    other = lax.ppermute(density, "pair", [(q, q ^ 1) for q in range(pairs)])
+    facing = jnp.where(
+        second,
+        jnp.stack([other[OWN - 1], density[OWN - 1]], axis=1),
+        jnp.stack([density[0], other[0]], axis=1),
+    )
+    facing, exponents, quartet_list = lax.optimization_barrier((facing, exponents, quartet_list))
+    ups = [(b * pairs + q, (b + 1) * pairs + q - 1) for b in range(count - 1) for q in range(1, pairs, 2)]
+    halo = lax.ppermute(facing, ("blk", "pair"), ups + [(high, low) for low, high in ups])
 
     tables = jnp.concatenate([exponents[None], offsets[None], expansion], axis=0)
     right, left = pl.pallas_call(
@@ -188,7 +203,12 @@
     listed = jnp.pad(quartet_list[0, 0], ((0, ROWS - 4), (0, 0)))
     listed += jnp.pad(list_length, ((4, ROWS - 5), (0, BS - 1)))
     payload = jnp.concatenate(
-        [low, density.reshape(OWN * BAND, ROWS, BS), high, listed.astype(jnp.bfloat16)[None]], axis=0
+        [
+            density.reshape(OWN * BAND, ROWS, BS),
+            halo.reshape(BAND * 2, ROWS, BS),
+            listed.astype(jnp.bfloat16)[None],
+        ],
+        axis=0,
     )
     payload, right, left = lax.optimization_barrier((payload, right, left))
     bank = lax.all_gather(payload, "pair", axis=0)

time: 38.6 us -> 37.7 us (0.977)
  the two profiles are of different devices: /device:TPU:31 before, /device:TPU:7 now
where the time goes in v4:
time: 37.7 us; the launch traced here: 37.4 us
  blocking collectives  25.8 us (68%)
  starting transfers between devices  5.8 us (15%)
  Pallas kernels  2.55 us (7%)
  other arithmetic  1.81 us (5%)
  between operations  0.73 us (2%)
  local copies, waits for them, and re-layouts  0.72 us (2%)
    all_gather x1, blocking collectives, shards(): bank = lax.all_gather(payload, 'pair', axis=0)  25.8 us
    ppermute x1, starting transfers between devices, shards(): lax.ppermute(facing, ('blk', 'pair'), ups + [(high, low) for low, high in...  3.1 us
    ppermute x1, starting transfers between devices, shards(): other = lax.ppermute(density, 'pair', [(q, q ^ 1) for q in range(pairs)])  2.7 us
    pallas_call x1, Pallas kernels, shards(): pl.pallas_call(products_kernel, out_shape=jax.ShapeDtypeStruct((OWN, BAND...  1.3 us
    pallas_call x1, Pallas kernels, shards(): pl.pallas_call(factors_kernel, out_shape=(jax.ShapeDtypeStruct((NEAR, 3 *...  1.24 us
    concatenate x1, other arithmetic, shards(): jnp.concatenate([exponents[None], offsets[None], expansion], axis=0)  1.09 us
  transfers between devices with their start and end apart: 2, of which 0 were waited for; matrix products, arithmetic and copies ran while one was open for 7% of the time, Pallas kernels for 3%

profile of v4, /device:TPU:7, one launch (start us, length us, event | category | flops | bytes accessed | tf_op | source)
XLA Modules:
  0.0 37.4 jit_solution(2899679422492255483)
XLA Ops:
  0.0 0.0 copy-start
  0.0 2.7 %collective-permute-start = (bf16[3,3,8,128]{3,2,1,0:T(8,128)(2,1)}, bf16[3,3,8,128]{3,2,1,0:T(8,128)(2,1)S(1)}, u32[]{:S(2)}, u32[]{:S(2)}) collective-permute-start(bf16[3,3,8,128]{3,2,1,0:T(8,128)(2,1)} %param.6), channel_id=1, source_target_pairs={{0,1},{1,0},{2,3},{3,2},{4,5},{5,4},{6,7},{7,6},{8,9},{9,8},{10,11... | collective-permute-start | bytes 55304 | tf_op jit(solution)/shard_map/ppermute | solution.py:178
  2.7 0.7 %slice_bitcast_fusion.3 = (bf16[3,1,8,128]{3,2,0,1:T(8,128)(2,1)S(1)}, bf16[3,1,8,128]{3,2,1,0:T(8,128)(2,1)S(1)}) fusion(bf16[3,3,8,128]{3,2,1,0:T(8,128)(2,1)} %param.6), kind=kLoop, calls=%fused_computation.7 | loop fusion | bytes 24576 | tf_op jit(solution)/shard_map/stack;squeeze | solution.py:181
  4.1 0.0 collective-permute-done
  4.1 3.1 %collective-permute-start.1 = (bf16[3,2,8,128]{3,2,1,0:T(8,128)(2,1)S(1)}, bf16[3,2,8,128]{3,2,1,0:T(8,128)(2,1)S(1)}, u32[]{:S(2)}, u32[]{:S(2)}) collective-permute-start(bf16[3,2,8,128]{3,2,1,0:T(8,128)(2,1)S(1)} %maximum_select_fusion), channel_id=1, source_target_pairs={{1,16},{3,18},{5,20},{7,22},{9,24},{11,26},{13,28},{15,30},{17,32}... | collective-permute-start | bytes 36872 | tf_op jit(solution)/shard_map/ppermute | solution.py:186
  7.2 1.1 %pad_maximum_fusion.table_ref = f32[6,12288]{1,0:T(8,128)S(1)} fusion(f32[4,12288]{1,0:T(4,128)} %param.9, f32[1,12288]{1,0:T(1,128)} %bitcast.18, f32[1,12288]{1,0:T(1,128)} %bitcast.19), kind=kLoop, calls=%fused_computation | loop fusion | flops 147456 | bytes 589824 | tf_op jit(solution)/shard_map/concatenate | solution.py:188
  8.3 0.7 %fusion = bf16[1,8,128]{2,1,0:T(8,128)(2,1)S(1)} fusion(s32[1,1]{1,0:T(1,128)S(6)} %copy.10, s32[4,128]{1,0:T(4,128)} %bitcast.21), kind=kLoop, calls=%fused_computation.9 | loop fusion | flops 2048 | bytes 4100 | tf_op jit(solution)/shard_map/broadcast_in_dim | solution.py:209
  9.0 1.2 %factors.1 = (bf16[5,1536,128]{2,1,0:T(8,128)(2,1)S(1)}, bf16[288,128]{1,0:T(8,128)(2,1)S(1)}) custom-call(f32[6,12288]{1,0:T(8,128)S(1)} %pad_maximum_fusion.table_ref), custom_call_target="tpu_custom_call" | custom-call | flops 30000000 | bytes 3000000 | tf_op jit(solution)/shard_map/factors/pallas_call | solution.py:189
  10.3 0.0 collective-permute-done.1
  10.3 0.0 copy-done
  10.3 25.8 %all-gather = bf16[256,8,128]{2,1,0:T(8,128)(2,1)S(1)} all-gather(bf16[16,8,128]{2,1,0:T(8,128)(2,1)S(1)} %pad_maximum_fusion.1), channel_id=2, replica_groups=mesh['blk'=32,'pair'=16] {'pair'}, dimensions={0}, use_global_device_ids=true | all-gather | bytes 557056 | tf_op jit(solution)/shard_map/all_gather | solution.py:214
  36.1 1.3 %products.1 = f32[3,3,8,128]{3,2,1,0:T(8,128)} custom-call(bf16[16,16,8,128]{3,2,1,0:T(8,128)(2,1)S(1)} %bitcast.16, f32[6,12288]{1,0:T(8,128)S(1)} %pad_maximum_fusion.table_ref, bf16[5,1536,128]{2,1,0:T(8,128)(2,1)S(1)} %get-tuple-element.19.right_in, bf16[288,128]{1,0:T(8,128)(2,1)S(1)} %get-tuple-element.20.left_in), custom_call_target="tpu_custom_call" | custom-call | tf_op jit(solution)/shard_map/products/pallas_call | solution.py:216
  (3 shorter events, 0.0 us)
Async XLA Ops:
  0.0 10.3 %copy-start = (bf16[3,3,8,128]{3,2,1,0:T(8,128)(2,1)S(1)}, bf16[3,3,8,128]{3,2,1,0:T(8,128)(2,1)}, u32[]{:S(2)}) copy-start(bf16[3,3,8,128]{3,2,1,0:T(8,128)(2,1)} %param.6) | copy-start | bytes 55300
  0.0 4.1 %collective-permute-start = (bf16[3,3,8,128]{3,2,1,0:T(8,128)(2,1)}, bf16[3,3,8,128]{3,2,1,0:T(8,128)(2,1)S(1)}, u32[]{:S(2)}, u32[]{:S(2)}) collective-permute-start(bf16[3,3,8,128]{3,2,1,0:T(8,128)(2,1)} %param.6), channel_id=1, source_target_pairs={{0,1},{1,0},{2,3},{3,2},{4,5},{5,4},{6,7},{7,6},{8,9},{9,8},{10,11... | collective-permute-start | bytes 55304 | tf_op jit(solution)/shard_map/ppermute | solution.py:178
  4.1 6.2 %collective-permute-start.1 = (bf16[3,2,8,128]{3,2,1,0:T(8,128)(2,1)S(1)}, bf16[3,2,8,128]{3,2,1,0:T(8,128)(2,1)S(1)}, u32[]{:S(2)}, u32[]{:S(2)}) collective-permute-start(bf16[3,2,8,128]{3,2,1,0:T(8,128)(2,1)S(1)} %maximum_select_fusion), channel_id=1, source_target_pairs={{1,16},{3,18},{5,20},{7,22},{9,24},{11,26},{13,28},{15,30},{17,32}... | collective-permute-start | bytes 36872 | tf_op jit(solution)/shard_map/ppermute | solution.py:186

commit v5 on v4

--- a/solution.py
+++ b/solution.py
@@ -13,6 +13,7 @@
 FAR = OWN + 4
 ROWS = 8
 SCALE = 0.0078125
+OWN_ROWS = (OWN * BAND + 1) * ROWS
 
 LEFT_PAIRS = [(k, i) for k in range(NEAR) for i in range(OWN) if abs(i - (k - 1)) <= 1]
 FIRST_LEFT = {pair: at for at, pair in enumerate(LEFT_PAIRS)}
@@ -29,16 +30,17 @@
 def make_factors(table_ref, right_ref, left_ref, rows_ref, cols_ref):
     own_first = lax.axis_index("blk") * OWN
     my_row = pl.multiple_of(lax.axis_index("pair") * ROWS, ROWS)
-    nblk = table_ref.shape[1] // BS
+    nblk = (table_ref.shape[0] - OWN_ROWS) // (2 + NAUX)
 
     rows_ref[...] = jnp.zeros_like(rows_ref)
     for t in range(FAR):
         block = jnp.clip(own_first - 2 + t, 0, nblk - 1)
-        values = table_ref[:, pl.ds(pl.multiple_of(block * BS, BS), BS)]
-        rows_ref[t : t + 1, :] = values[0:1, :]
-        rows_ref[8 + t : 9 + t, :] = 2.0 * block.astype(jnp.float32) + values[1:2, :]
+        rows_ref[t : t + 1, :] = table_ref[pl.ds(block, 1), :]
+        offset = table_ref[pl.ds(nblk + block, 1), :]
+        rows_ref[8 + t : 9 + t, :] = 2.0 * block.astype(jnp.float32) + offset
         for p in range(NAUX):
-            rows_ref[16 + 8 * p + t : 17 + 8 * p + t, :] = values[2 + p : 3 + p, :]
+            weight = table_ref[pl.ds(2 * nblk + NAUX * block + p, 1), :]
+            rows_ref[16 + 8 * p + t : 17 + 8 * p + t, :] = weight
     cols_ref[...] = rows_ref[...].T
 
     def tiles(columns, t_row, t_col):
@@ -104,13 +106,13 @@
             pieces = [bank_ref[q, (near - 1) * BAND + c] for q in range(devices)]
         else:
             holder = 0 if near == 0 else 1
-            pieces = [bank_ref[q // 2 * 2 + holder, OWN * BAND + 2 * c + q % 2] for q in range(devices)]
+            pieces = [bank_ref[q // 2 * 2 + holder, OWN * BAND + 1 + 2 * c + q % 2] for q in range(devices)]
         return jnp.concatenate([piece.astype(jnp.float32) for piece in pieces], axis=0)
 
     own_first = lax.axis_index("blk") * OWN
     slot = lax.broadcasted_iota(jnp.int32, (1, BS), 1)
     code_row = lax.broadcasted_iota(jnp.int32, (BS, BS), 0)
-    lists = bank_ref[:, NEAR * BAND].astype(jnp.float32).astype(jnp.int32)
+    lists = bank_ref[:, OWN * BAND].astype(jnp.float32).astype(jnp.int32)
     found = jnp.zeros((BS, BS), jnp.float32)
     for q in range(lists.shape[0]):
         row_b, col_b, mid_b, far_b = (lists[q, n : n + 1, :] for n in range(4))
@@ -176,16 +178,31 @@
     second = (lax.axis_index("pair") & 1) == 1
 
     other = lax.ppermute(density, "pair", [(q, q ^ 1) for q in range(pairs)])
+
+    nblk = exponents.shape[0] // BS
+    pieces = [
+        exponents.reshape(nblk, BS),
+        offsets.reshape(nblk, BS),
+        expansion.reshape(NAUX, nblk, BS).transpose(1, 0, 2).reshape(NAUX * nblk, BS),
+        density.reshape(OWN * BAND * ROWS, BS),
+        quartet_list[0, 0],
+        list_length,
+    ]
+    rows, tables, at = (2 + NAUX) * nblk + OWN_ROWS, 0.0, 0
+    for piece in pieces:
+        high, wide = piece.shape
+        tables += jnp.pad(piece, ((at, rows - at - high), (0, BS - wide))).astype(jnp.float32)
+        at += high
+    tables = lax.optimization_barrier(tables)
+    own = tables[-OWN_ROWS:].astype(jnp.bfloat16).reshape(OWN * BAND + 1, ROWS, BS)
     facing = jnp.where(
         second,
-        jnp.stack([other[OWN - 1], density[OWN - 1]], axis=1),
-        jnp.stack([density[0], other[0]], axis=1),
+        jnp.stack([other[OWN - 1], own[(OWN - 1) * BAND : OWN * BAND]], axis=1),
+        jnp.stack([own[:BAND], other[0]], axis=1),
     )
-    facing, exponents, quartet_list = lax.optimization_barrier((facing, exponents, quartet_list))
     ups = [(b * pairs + q, (b + 1) * pairs + q - 1) for b in range(count - 1) for q in range(1, pairs, 2)]
     halo = lax.ppermute(facing, ("blk", "pair"), ups + [(high, low) for low, high in ups])
 
-    tables = jnp.concatenate([exponents[None], offsets[None], expansion], axis=0)
     right, left = pl.pallas_call(
         factors_kernel,
         out_shape=(
@@ -200,16 +217,7 @@
         name="factors",
     )(tables)
 
-    listed = jnp.pad(quartet_list[0, 0], ((0, ROWS - 4), (0, 0)))
-    listed += jnp.pad(list_length, ((4, ROWS - 5), (0, BS - 1)))
-    payload = jnp.concatenate(
-        [
-            density.reshape(OWN * BAND, ROWS, BS),
-            halo.reshape(BAND * 2, ROWS, BS),
-            listed.astype(jnp.bfloat16)[None],
-        ],
-        axis=0,
-    )
+    payload = jnp.concatenate([own, halo.reshape(BAND * 2, ROWS, BS)], axis=0)
     payload, right, left = lax.optimization_barrier((payload, right, left))
     bank = lax.all_gather(payload, "pair", axis=0)
 

time: 37.7 us -> 37.3 us (0.989)
  other arithmetic: 1.81 us -> 1.01 us
  local copies, waits for them, and re-layouts: 0.72 us -> 0.01 us
  blocking collectives: 25.8 us -> 26.5 us
  waiting for transfers between devices: 0.01 us -> 0.63 us
    concatenate x2 -> x1, other arithmetic: 1.1 us -> 0.01 us  [shards(): payload = jnp.concatenate([own, halo.reshape(BAND * 2, ROWS, BS)], axis=0)]
    add x0 -> x1, other arithmetic: none -> 0.97 us  [shards(): tables += jnp.pad(piece, ((at, rows - at - high), (0, BS - wide))).astype...]
    all_gather x1, blocking collectives: 25.8 us -> 26.5 us  [shards(): bank = lax.all_gather(payload, 'pair', axis=0)]
    another operation x2, local copies, waits for them, and re-layouts: 0.72 us -> 0.01 us  [shards(): jnp.stack([other[OWN - 1], own[(OWN - 1) * BAND:OWN * BAND]], axis=1)]
    broadcast_in_dim x1 -> x0, other arithmetic: 0.7 us -> none  [shards(): listed.astype(jnp.bfloat16)[None]]
    ppermute x1, waiting for transfers between devices: 0.01 us -> 0.62 us  [shards(): lax.ppermute(facing, ('blk', 'pair'), ups + [(high, low) for low, high in...]
  transfers between devices with their start and end apart: 2 -> 2, of which waited for: 0 -> 1; matrix products, arithmetic and copies ran while one was open for 7% -> 3% of each run, Pallas kernels for 3% -> 3%
where the time goes in v5:
time: 37.3 us; the launch traced here: 37.1 us
  blocking collectives  26.5 us (71%)
  starting transfers between devices  5.67 us (15%)
  Pallas kernels  2.56 us (7%)
  other arithmetic  1.01 us (3%)
  between operations  0.72 us (2%)
  waiting for transfers between devices  0.63 us (2%)
    all_gather x1, blocking collectives, shards(): bank = lax.all_gather(payload, 'pair', axis=0)  26.5 us
    ppermute x1, starting transfers between devices, shards(): lax.ppermute(facing, ('blk', 'pair'), ups + [(high, low) for low, high in...  3.1 us
    ppermute x1, starting transfers between devices, shards(): other = lax.ppermute(density, 'pair', [(q, q ^ 1) for q in range(pairs)])  2.57 us
    pallas_call x1, Pallas kernels, shards(): pl.pallas_call(products_kernel, out_shape=jax.ShapeDtypeStruct((OWN, BAND...  1.3 us
    pallas_call x1, Pallas kernels, shards(): pl.pallas_call(factors_kernel, out_shape=(jax.ShapeDtypeStruct((NEAR, 3 *...  1.26 us
    add x1, other arithmetic, shards(): tables += jnp.pad(piece, ((at, rows - at - high), (0, BS - wide))).astype...  0.97 us
  transfers between devices with their start and end apart: 2, of which 1 were waited for; matrix products, arithmetic and copies ran while one was open for 3% of the time, Pallas kernels for 3%

profile of v5, /device:TPU:7, one launch (start us, length us, event | category | flops | bytes accessed | tf_op | source)
XLA Modules:
  0.0 37.1 jit_solution(11048094559538582724)
XLA Ops:
  0.0 2.6 %collective-permute-start = (bf16[3,3,8,128]{3,2,1,0:T(8,128)(2,1)}, bf16[3,3,8,128]{3,2,1,0:T(8,128)(2,1)S(1)}, u32[]{:S(2)}, u32[]{:S(2)}) collective-permute-start(bf16[3,3,8,128]{3,2,1,0:T(8,128)(2,1)} %param.6), channel_id=1, source_target_pairs={{0,1},{1,0},{2,3},{3,2},{4,5},{5,4},{6,7},{7,6},{8,9},{9,8},{10,11... | collective-permute-start | bytes 55304 | tf_op jit(solution)/shard_map/ppermute | solution.py:180
  3.2 1.0 %convert_add_fusion.table_ref = f32[656,128]{1,0:T(8,128)S(1)} fusion(s32[1,1]{1,0:T(1,128)S(6)} %copy.15, s32[4,128]{1,0:T(4,128)} %bitcast.29, f32[384,128]{1,0:T(8,128)} %bitcast.24, f32[96,128]{1,0:T(8,128)} %bitcast.25, f32[96,128]{1,0:T(8,128)} %bitcast.26, bf16[72,128]{1,0:T(8,128)(2,1)} %bitcast.27), kind=kLoop, calls=%fused_computation | loop fusion | flops 671744 | bytes 651268 | tf_op jit(solution)/shard_map/add | solution.py:194
  4.2 0.0 collective-permute-done
  4.3 3.1 %collective-permute-start.1 = (bf16[3,2,8,128]{3,2,1,0:T(8,128)(2,1)S(1)}, bf16[3,2,8,128]{3,2,1,0:T(8,128)(2,1)S(1)}, u32[]{:S(2)}, u32[]{:S(2)}) collective-permute-start(bf16[3,2,8,128]{3,2,1,0:T(8,128)(2,1)S(1)} %maximum_select_fusion), channel_id=1, source_target_pairs={{1,16},{3,18},{5,20},{7,22},{9,24},{11,26},{13,28},{15,30},{17,32}... | collective-permute-start | bytes 36872 | tf_op jit(solution)/shard_map/ppermute | solution.py:204
  7.4 1.3 %factors.1 = (bf16[5,1536,128]{2,1,0:T(8,128)(2,1)S(1)}, bf16[288,128]{1,0:T(8,128)(2,1)S(1)}) custom-call(f32[656,128]{1,0:T(8,128)S(1)} %convert_add_fusion.table_ref), custom_call_target="tpu_custom_call" | custom-call | flops 30000000 | bytes 3000000 | tf_op jit(solution)/shard_map/factors/pallas_call | solution.py:206
  8.7 0.6 %collective-permute-done.1 = bf16[3,2,8,128]{3,2,1,0:T(8,128)(2,1)S(1)} collective-permute-done((bf16[3,2,8,128]{3,2,1,0:T(8,128)(2,1)S(1)}, bf16[3,2,8,128]{3,2,1,0:T(8,128)(2,1)S(1)}, u32[]{:S(2)}, u32[]{:S(2)}) %collective-permute-start.1) | collective-permute-done | bytes 12320 | tf_op jit(solution)/shard_map/ppermute | solution.py:204
  9.3 26.5 %all-gather = bf16[256,8,128]{2,1,0:T(8,128)(2,1)S(1)} all-gather(bf16[16,8,128]{2,1,0:T(8,128)(2,1)S(1)} %pad_maximum_fusion), channel_id=2, replica_groups=mesh['blk'=32,'pair'=16] {'pair'}, dimensions={0}, use_global_device_ids=true | all-gather | bytes 557056 | tf_op jit(solution)/shard_map/all_gather | solution.py:222
  35.8 1.3 %products.1 = f32[3,3,8,128]{3,2,1,0:T(8,128)} custom-call(bf16[16,16,8,128]{3,2,1,0:T(8,128)(2,1)S(1)} %bitcast.23, f32[656,128]{1,0:T(8,128)S(1)} %convert_add_fusion.table_ref, bf16[5,1536,128]{2,1,0:T(8,128)(2,1)S(1)} %get-tuple-element.13.right_in, bf16[288,128]{1,0:T(8,128)(2,1)S(1)} %get-tuple-element.14.left_in), custom_call_target="tpu_custom_call" | custom-call | tf_op jit(solution)/shard_map/products/pallas_call | solution.py:224
  (6 shorter events, 0.0 us)
Async XLA Ops:
  0.0 4.2 %collective-permute-start = (bf16[3,3,8,128]{3,2,1,0:T(8,128)(2,1)}, bf16[3,3,8,128]{3,2,1,0:T(8,128)(2,1)S(1)}, u32[]{:S(2)}, u32[]{:S(2)}) collective-permute-start(bf16[3,3,8,128]{3,2,1,0:T(8,128)(2,1)} %param.6), channel_id=1, source_target_pairs={{0,1},{1,0},{2,3},{3,2},{4,5},{5,4},{6,7},{7,6},{8,9},{9,8},{10,11... | collective-permute-start | bytes 55304 | tf_op jit(solution)/shard_map/ppermute | solution.py:180
  4.3 5.0 %collective-permute-start.1 = (bf16[3,2,8,128]{3,2,1,0:T(8,128)(2,1)S(1)}, bf16[3,2,8,128]{3,2,1,0:T(8,128)(2,1)S(1)}, u32[]{:S(2)}, u32[]{:S(2)}) collective-permute-start(bf16[3,2,8,128]{3,2,1,0:T(8,128)(2,1)S(1)} %maximum_select_fusion), channel_id=1, source_target_pairs={{1,16},{3,18},{5,20},{7,22},{9,24},{11,26},{13,28},{15,30},{17,32}... | collective-permute-start | bytes 36872 | tf_op jit(solution)/shard_map/ppermute | solution.py:204

commit v6 on v5

--- a/solution.py
+++ b/solution.py
@@ -21,6 +21,10 @@
 
 def owners_of(near):
     return [i for i in range(OWN) if abs(i - (near - 1)) <= 1]
+
+
+def holds_above(q):
+    return ((lax.axis_index("blk") + q) & 1) == 0
 
 
 def early():
@@ -105,7 +109,7 @@
         if 0 < near < NEAR - 1:
             pieces = [bank_ref[q, (near - 1) * BAND + c] for q in range(devices)]
         else:
-            holder = 0 if near == 0 else 1
+            holder = jnp.where(holds_above(0), 1, 0) if near == 0 else jnp.where(holds_above(0), 0, 1)
             pieces = [bank_ref[q // 2 * 2 + holder, OWN * BAND + 1 + 2 * c + q % 2] for q in range(devices)]
         return jnp.concatenate([piece.astype(jnp.float32) for piece in pieces], axis=0)
 
@@ -176,6 +180,7 @@
     count = lax.axis_size("blk")
     pairs = lax.axis_size("pair")
     second = (lax.axis_index("pair") & 1) == 1
+    up = holds_above(lax.axis_index("pair"))
 
     other = lax.ppermute(density, "pair", [(q, q ^ 1) for q in range(pairs)])
 
@@ -195,12 +200,12 @@
         at += high
     tables = lax.optimization_barrier(tables)
     own = tables[-OWN_ROWS:].astype(jnp.bfloat16).reshape(OWN * BAND + 1, ROWS, BS)
-    facing = jnp.where(
-        second,
-        jnp.stack([other[OWN - 1], own[(OWN - 1) * BAND : OWN * BAND]], axis=1),
-        jnp.stack([own[:BAND], other[0]], axis=1),
-    )
-    ups = [(b * pairs + q, (b + 1) * pairs + q - 1) for b in range(count - 1) for q in range(1, pairs, 2)]
+    mine = jnp.where(up, own[(OWN - 1) * BAND : OWN * BAND], own[:BAND])
+    theirs = jnp.where(up, other[OWN - 1], other[0])
+    facing = jnp.where(second, jnp.stack([theirs, mine], axis=1), jnp.stack([mine, theirs], axis=1))
+    ups = [
+        (b * pairs + q, (b + 1) * pairs + q) for b in range(count - 1) for q in range(pairs) if (b + q) % 2 == 0
+    ]
     halo = lax.ppermute(facing, ("blk", "pair"), ups + [(high, low) for low, high in ups])
 
     right, left = pl.pallas_call(

time: 37.3 us -> 36.6 us (0.981)
  the two profiles are of different devices: /device:TPU:7 before, /device:TPU:1 now
where the time goes in v6:
time: 36.6 us; the launch traced here: 36.4 us
  blocking collectives  22.7 us (62%)
  starting transfers between devices  9.44 us (26%)
  Pallas kernels  2.55 us (7%)
  other arithmetic  1.02 us (3%)
  between operations  0.75 us (2%)
    all_gather x1, blocking collectives, shards(): bank = lax.all_gather(payload, 'pair', axis=0)  22.7 us
    ppermute x1, starting transfers between devices, shards(): other = lax.ppermute(density, 'pair', [(q, q ^ 1) for q in range(pairs)])  8.77 us
    pallas_call x1, Pallas kernels, shards(): pl.pallas_call(products_kernel, out_shape=jax.ShapeDtypeStruct((OWN, BAND...  1.29 us
    pallas_call x1, Pallas kernels, shards(): pl.pallas_call(factors_kernel, out_shape=(jax.ShapeDtypeStruct((NEAR, 3 *...  1.26 us
    add x1, other arithmetic, shards(): tables += jnp.pad(piece, ((at, rows - at - high), (0, BS - wide))).astype...  0.97 us
  transfers between devices with their start and end apart: 2, of which 0 were waited for; matrix products, arithmetic and copies ran while one was open for 3% of the time, Pallas kernels for 3%

profile of v6, /device:TPU:1, one launch (start us, length us, event | category | flops | bytes accessed | tf_op | source)
XLA Modules:
  0.0 36.4 jit_solution(13311437930295593775)
XLA Ops:
  0.0 8.8 %collective-permute-start = (bf16[3,3,8,128]{3,2,1,0:T(8,128)(2,1)}, bf16[3,3,8,128]{3,2,1,0:T(8,128)(2,1)S(1)}, u32[]{:S(2)}, u32[]{:S(2)}) collective-permute-start(bf16[3,3,8,128]{3,2,1,0:T(8,128)(2,1)} %param.6), channel_id=1, source_target_pairs={{0,1},{1,0},{2,3},{3,2},{4,5},{5,4},{6,7},{7,6},{8,9},{9,8},{10,11... | collective-permute-start | bytes 55304 | tf_op jit(solution)/shard_map/ppermute | solution.py:185
  9.4 1.0 %convert_add_fusion.table_ref = f32[656,128]{1,0:T(8,128)S(1)} fusion(s32[1,1]{1,0:T(1,128)S(6)} %copy.14, s32[4,128]{1,0:T(4,128)} %bitcast.25, f32[384,128]{1,0:T(8,128)} %bitcast.20, f32[96,128]{1,0:T(8,128)} %bitcast.21, f32[96,128]{1,0:T(8,128)} %bitcast.22, bf16[72,128]{1,0:T(8,128)(2,1)} %bitcast.23), kind=kLoop, calls=%fused_computation | loop fusion | flops 671744 | bytes 651268 | tf_op jit(solution)/shard_map/add | solution.py:199
  10.5 0.0 collective-permute-done
  10.5 0.7 %collective-permute-start.1 = (bf16[3,2,8,128]{3,2,1,0:T(8,128)(2,1)S(1)}, bf16[3,2,8,128]{3,2,1,0:T(8,128)(2,1)S(1)}, u32[]{:S(2)}, u32[]{:S(2)}) collective-permute-start(bf16[3,2,8,128]{3,2,1,0:T(8,128)(2,1)S(1)} %maximum_select_fusion), channel_id=1, source_target_pairs={{0,16},{2,18},{4,20},{6,22},{8,24},{10,26},{12,28},{14,30},{17,33}... | collective-permute-start | bytes 36872 | tf_op jit(solution)/shard_map/ppermute | solution.py:209
  11.2 1.3 %factors.1 = (bf16[5,1536,128]{2,1,0:T(8,128)(2,1)S(1)}, bf16[288,128]{1,0:T(8,128)(2,1)S(1)}) custom-call(f32[656,128]{1,0:T(8,128)S(1)} %convert_add_fusion.table_ref), custom_call_target="tpu_custom_call" | custom-call | flops 30000000 | bytes 3000000 | tf_op jit(solution)/shard_map/factors/pallas_call | solution.py:211
  12.4 0.0 collective-permute-done.1
  12.5 22.7 %all-gather = bf16[256,8,128]{2,1,0:T(8,128)(2,1)S(1)} all-gather(bf16[16,8,128]{2,1,0:T(8,128)(2,1)S(1)} %pad_maximum_fusion), channel_id=2, replica_groups=mesh['blk'=32,'pair'=16] {'pair'}, dimensions={0}, use_global_device_ids=true | all-gather | bytes 557056 | tf_op jit(solution)/shard_map/all_gather | solution.py:227
  35.1 1.3 %products.1 = f32[3,3,8,128]{3,2,1,0:T(8,128)} custom-call(bf16[16,16,8,128]{3,2,1,0:T(8,128)(2,1)S(1)} %bitcast.19, f32[656,128]{1,0:T(8,128)S(1)} %convert_add_fusion.table_ref, bf16[5,1536,128]{2,1,0:T(8,128)(2,1)S(1)} %get-tuple-element.13.right_in, bf16[288,128]{1,0:T(8,128)(2,1)S(1)} %get-tuple-element.14.left_in), custom_call_target="tpu_custom_call" | custom-call | tf_op jit(solution)/shard_map/products/pallas_call | solution.py:229
  (6 shorter events, 0.1 us)
Async XLA Ops:
  0.0 10.5 %collective-permute-start = (bf16[3,3,8,128]{3,2,1,0:T(8,128)(2,1)}, bf16[3,3,8,128]{3,2,1,0:T(8,128)(2,1)S(1)}, u32[]{:S(2)}, u32[]{:S(2)}) collective-permute-start(bf16[3,3,8,128]{3,2,1,0:T(8,128)(2,1)} %param.6), channel_id=1, source_target_pairs={{0,1},{1,0},{2,3},{3,2},{4,5},{5,4},{6,7},{7,6},{8,9},{9,8},{10,11... | collective-permute-start | bytes 55304 | tf_op jit(solution)/shard_map/ppermute | solution.py:185
  10.5 2.0 %collective-permute-start.1 = (bf16[3,2,8,128]{3,2,1,0:T(8,128)(2,1)S(1)}, bf16[3,2,8,128]{3,2,1,0:T(8,128)(2,1)S(1)}, u32[]{:S(2)}, u32[]{:S(2)}) collective-permute-start(bf16[3,2,8,128]{3,2,1,0:T(8,128)(2,1)S(1)} %maximum_select_fusion), channel_id=1, source_target_pairs={{0,16},{2,18},{4,20},{6,22},{8,24},{10,26},{12,28},{14,30},{17,33}... | collective-permute-start | bytes 36872 | tf_op jit(solution)/shard_map/ppermute | solution.py:209

commit v7 on v6

--- a/solution.py
+++ b/solution.py
@@ -184,6 +184,13 @@
 
     other = lax.ppermute(density, "pair", [(q, q ^ 1) for q in range(pairs)])
 
+    mine = jnp.where(up, density[OWN - 1], density[0])
+    theirs = jnp.where(up, other[OWN - 1], other[0])
+    facing = jnp.where(second, jnp.stack([theirs, mine], axis=1), jnp.stack([mine, theirs], axis=1))
+    facing, exponents, offsets, expansion, quartet_list = lax.optimization_barrier(
+        (facing, exponents, offsets, expansion, quartet_list)
+    )
+
     nblk = exponents.shape[0] // BS
     pieces = [
         exponents.reshape(nblk, BS),
@@ -200,9 +207,6 @@
         at += high
     tables = lax.optimization_barrier(tables)
     own = tables[-OWN_ROWS:].astype(jnp.bfloat16).reshape(OWN * BAND + 1, ROWS, BS)
-    mine = jnp.where(up, own[(OWN - 1) * BAND : OWN * BAND], own[:BAND])
-    theirs = jnp.where(up, other[OWN - 1], other[0])
-    facing = jnp.where(second, jnp.stack([theirs, mine], axis=1), jnp.stack([mine, theirs], axis=1))
     ups = [
         (b * pairs + q, (b + 1) * pairs + q) for b in range(count - 1) for q in range(pairs) if (b + q) % 2 == 0
     ]

time: 36.6 us -> 36.4 us (level)
  blocking collectives: 22.7 us -> 21.7 us
  other arithmetic: 1.02 us -> 1.72 us
    all_gather x1, blocking collectives: 22.7 us -> 21.7 us  [shards(): bank = lax.all_gather(payload, 'pair', axis=0)]
    select_n x1, other arithmetic: 0.01 us -> 0.72 us  [shards(): mine = jnp.where(up, density[OWN - 1], density[0])]
  transfers between devices with their start and end apart: 2 -> 2, of which waited for: 0 -> 0; matrix products, arithmetic and copies ran while one was open for 3% -> 5% of each run, Pallas kernels for 3% -> 3%
where the time goes in v7:
time: 36.4 us; the launch traced here: 36.2 us
  blocking collectives  21.7 us (60%)
  starting transfers between devices  9.44 us (26%)
  Pallas kernels  2.6 us (7%)
  other arithmetic  1.72 us (5%)
  between operations  0.73 us (2%)
    all_gather x1, blocking collectives, shards(): bank = lax.all_gather(payload, 'pair', axis=0)  21.7 us
    ppermute x1, starting transfers between devices, shards(): other = lax.ppermute(density, 'pair', [(q, q ^ 1) for q in range(pairs)])  8.78 us
    pallas_call x1, Pallas kernels, shards(): pl.pallas_call(products_kernel, out_shape=jax.ShapeDtypeStruct((OWN, BAND...  1.34 us
    pallas_call x1, Pallas kernels, shards(): pl.pallas_call(factors_kernel, out_shape=(jax.ShapeDtypeStruct((NEAR, 3 *...  1.26 us
    add x1, other arithmetic, shards(): tables += jnp.pad(piece, ((at, rows - at - high), (0, BS - wide))).astype...  0.97 us
  transfers between devices with their start and end apart: 2, of which 0 were waited for; matrix products, arithmetic and copies ran while one was open for 5% of the time, Pallas kernels for 3%

profile of v7, /device:TPU:1, one launch (start us, length us, event | category | flops | bytes accessed | tf_op | source)
XLA Modules:
  0.0 36.2 jit_solution(1615613358587344635)
XLA Ops:
  0.0 8.8 %collective-permute-start = (bf16[3,3,8,128]{3,2,1,0:T(8,128)(2,1)}, bf16[3,3,8,128]{3,2,1,0:T(8,128)(2,1)S(1)}, u32[]{:S(2)}, u32[]{:S(2)}) collective-permute-start(bf16[3,3,8,128]{3,2,1,0:T(8,128)(2,1)} %param.6), channel_id=1, source_target_pairs={{0,1},{1,0},{2,3},{3,2},{4,5},{5,4},{6,7},{7,6},{8,9},{9,8},{10,11... | collective-permute-start | bytes 55304 | tf_op jit(solution)/shard_map/ppermute | solution.py:185
  8.8 0.7 %select_bitcast_fusion = bf16[3,1,8,128]{3,2,1,0:T(8,128)(2,1)S(1)} fusion(bf16[3,3,8,128]{3,2,1,0:T(8,128)(2,1)} %param.6, pred[]{:T(512)S(6)} %eq.7), kind=kLoop, calls=%fused_computation.7 | loop fusion | flops 3072 | bytes 18433 | tf_op jit(solution)/shard_map/jit(_where)/select_n | solution.py:187
  10.2 0.0 collective-permute-done
  10.2 0.7 %collective-permute-start.1 = (bf16[3,2,8,128]{3,2,1,0:T(8,128)(2,1)S(1)}, bf16[3,2,8,128]{3,2,1,0:T(8,128)(2,1)S(1)}, u32[]{:S(2)}, u32[]{:S(2)}) collective-permute-start(bf16[3,2,8,128]{3,2,1,0:T(8,128)(2,1)S(1)} %maximum_select_fusion), channel_id=1, source_target_pairs={{0,16},{2,18},{4,20},{6,22},{8,24},{10,26},{12,28},{14,30},{17,33}... | collective-permute-start | bytes 36872 | tf_op jit(solution)/shard_map/ppermute | solution.py:213
  10.9 1.0 %convert_add_fusion.table_ref = f32[656,128]{1,0:T(8,128)S(1)} fusion(s32[1,1]{1,0:T(1,128)S(6)} %copy.10, s32[4,128]{1,0:T(4,128)} %bitcast.23, f32[384,128]{1,0:T(8,128)} %bitcast.18, f32[96,128]{1,0:T(8,128)} %bitcast.20, f32[96,128]{1,0:T(8,128)} %bitcast.21, bf16[72,128]{1,0:T(8,128)(2,1)} %bitcast.19), kind=kLoop, calls=%fused_computation | loop fusion | flops 671744 | bytes 651268 | tf_op jit(solution)/shard_map/add | solution.py:206
  11.9 1.3 %factors.1 = (bf16[5,1536,128]{2,1,0:T(8,128)(2,1)S(1)}, bf16[288,128]{1,0:T(8,128)(2,1)S(1)}) custom-call(f32[656,128]{1,0:T(8,128)S(1)} %convert_add_fusion.table_ref), custom_call_target="tpu_custom_call" | custom-call | flops 30000000 | bytes 3000000 | tf_op jit(solution)/shard_map/factors/pallas_call | solution.py:215
  13.1 0.0 collective-permute-done.1
  13.2 21.7 %all-gather = bf16[256,8,128]{2,1,0:T(8,128)(2,1)S(1)} all-gather(bf16[16,8,128]{2,1,0:T(8,128)(2,1)S(1)} %pad_maximum_fusion), channel_id=2, replica_groups=mesh['blk'=32,'pair'=16] {'pair'}, dimensions={0}, use_global_device_ids=true | all-gather | bytes 557056 | tf_op jit(solution)/shard_map/all_gather | solution.py:231
  34.8 1.3 %products.1 = f32[3,3,8,128]{3,2,1,0:T(8,128)} custom-call(bf16[16,16,8,128]{3,2,1,0:T(8,128)(2,1)S(1)} %bitcast.17, f32[656,128]{1,0:T(8,128)S(1)} %convert_add_fusion.table_ref, bf16[5,1536,128]{2,1,0:T(8,128)(2,1)S(1)} %get-tuple-element.23.right_in, bf16[288,128]{1,0:T(8,128)(2,1)S(1)} %get-tuple-element.24.left_in), custom_call_target="tpu_custom_call" | custom-call | tf_op jit(solution)/shard_map/products/pallas_call | solution.py:233
  (4 shorter events, 0.0 us)
Async XLA Ops:
  0.0 10.2 %collective-permute-start = (bf16[3,3,8,128]{3,2,1,0:T(8,128)(2,1)}, bf16[3,3,8,128]{3,2,1,0:T(8,128)(2,1)S(1)}, u32[]{:S(2)}, u32[]{:S(2)}) collective-permute-start(bf16[3,3,8,128]{3,2,1,0:T(8,128)(2,1)} %param.6), channel_id=1, source_target_pairs={{0,1},{1,0},{2,3},{3,2},{4,5},{5,4},{6,7},{7,6},{8,9},{9,8},{10,11... | collective-permute-start | bytes 55304 | tf_op jit(solution)/shard_map/ppermute | solution.py:185
  10.2 2.9 %collective-permute-start.1 = (bf16[3,2,8,128]{3,2,1,0:T(8,128)(2,1)S(1)}, bf16[3,2,8,128]{3,2,1,0:T(8,128)(2,1)S(1)}, u32[]{:S(2)}, u32[]{:S(2)}) collective-permute-start(bf16[3,2,8,128]{3,2,1,0:T(8,128)(2,1)S(1)} %maximum_select_fusion), channel_id=1, source_target_pairs={{0,16},{2,18},{4,20},{6,22},{8,24},{10,26},{12,28},{14,30},{17,33}... | collective-permute-start | bytes 36872 | tf_op jit(solution)/shard_map/ppermute | solution.py:213
